TPU v7x, 256 devices: a whole 4x4x8 slice. The times are simulated.
256 devices in a mesh: replica: 4 (over x), shard: 64 (over y, z, core).
Axes of the slice: x: 4, y: 4, z: 8, core: 2. Of those that a mesh axis runs over, the one named last changes fastest.
Arguments:
- grads: bfloat16 [4, 32768, 2048], P('replica', 'shard'), may hold values from -3 to 3
- block_owner: int32 [256], replicated, may hold values from 0 to 511, as said below
- block_offsets: int32 [256, 2], replicated, may hold values from 0 to 32256, as said below
- stat_left: float32 [512, 512, 512], P(('replica', 'shard'))
- stat_right: float32 [512, 512, 512], P(('replica', 'shard'))
- root_left: bfloat16 [512, 512, 512], P(('replica', 'shard'))
- root_right: bfloat16 [512, 512, 512], P(('replica', 'shard'))
Outputs:
- new_left: float32 [512, 512, 512], P(('replica', 'shard'))
- new_right: float32 [512, 512, 512], P(('replica', 'shard'))
- direction: bfloat16 [32768, 2048], P('shard', 'replica')
Inputs may be any that keep to these rules, and one draw needn't show every extreme that they name: `block_owner`: values are distinct; value // 2 is the owning device, replica index times 64 plus shard index, and value % 2 its slot; some owner holds 2 blocks in every draw; the first slot of the first device and the last slot of the last device are used in every draw. `block_offsets`: multiples of 512; the blocks cover the window of 32768 x 2048 once.
All inputs are finite; a program needn't handle non-finite values.
Results may differ from a plain program's by a relative error of at most 0.017.
Values may be sent and summed in bfloat16 or wider, within the bound.
No kernel may reach another device: no remote copies, remote signals or barrier semaphores. Data moves between devices by JAX's collectives and lax.ppermute only.
A program may use at most 128 MiB of HBM per device.

v0:
```python
import jax
import jax.numpy as jnp
from jax import lax
from jax.sharding import PartitionSpec as P


def on_device(grads, block_owner, block_offsets, stat_left, stat_right, root_left, root_right):
    shards = lax.axis_size("shard")
    replicas = lax.axis_size("replica")
    slots = stat_left.shape[0]
    width = stat_left.shape[1]
    ncols = grads.shape[2] // width
    strip = width // shards
    blocks = block_owner.shape[0]
    positions = block_offsets[:, 0] // width * ncols + block_offsets[:, 1] // width
    owner_hot = (
        block_owner[:, None] == jnp.arange(replicas * shards * slots, dtype=jnp.int32)[None, :]
    ).astype(jnp.bfloat16)
    place_hot = (positions[:, None] == jnp.arange(blocks, dtype=jnp.int32)[None, :]).astype(
        jnp.bfloat16
    )
    select = jnp.dot(owner_hot.T, place_hot, preferred_element_type=jnp.float32).astype(
        jnp.bfloat16
    )
    select = select.reshape(replicas, shards, slots, shards, ncols)
    here = lax.dynamic_index_in_dim(select, lax.axis_index("replica"), 0, keepdims=False)
    total = lax.psum(grads[0].astype(jnp.float32).astype(jnp.bfloat16), "replica")
    parts = total.reshape(shards, strip, ncols, width)
    arrived = lax.all_to_all(parts, "shard", split_axis=0, concat_axis=0, tiled=True)
    outgoing = jnp.einsum(
        "skij,iajc->skac", here, arrived, preferred_element_type=jnp.float32
    ).astype(jnp.bfloat16)
    owned = lax.all_to_all(outgoing, "shard", split_axis=0, concat_axis=2, tiled=True)[0]
    gram_left = jnp.einsum("kab,kcb->kac", owned, owned, preferred_element_type=jnp.float32)
    gram_right = jnp.einsum("kba,kbc->kac", owned, owned, preferred_element_type=jnp.float32)
    new_left = stat_left + gram_left / width
    new_right = stat_right + gram_right / width
    right_side = jnp.einsum(
        "kab,kbc->kac", owned, root_right, preferred_element_type=jnp.float32
    ).astype(jnp.bfloat16)
    steer = jnp.einsum(
        "kab,kbc->kac", root_left, right_side, preferred_element_type=jnp.float32
    ).astype(jnp.bfloat16)
    pieces = steer.reshape(slots, shards, strip, width)
    returned = lax.all_to_all(pieces, "shard", split_axis=1, concat_axis=1, tiled=True)
    placed = jnp.einsum("skij,ksac->iajc", here, returned, preferred_element_type=jnp.float32)
    filled = lax.psum_scatter(
        placed.astype(jnp.bfloat16), "replica", scatter_dimension=2, tiled=True
    )
    home = lax.all_to_all(filled, "shard", split_axis=0, concat_axis=1, tiled=True)
    direction = home.reshape(width, home.shape[2] * width)
    return (new_left, new_right, direction)


def solution(mesh):
    placed = (
        P("replica", "shard", None),
        P(),
        P(),
        P(("replica", "shard"), None, None),
        P(("replica", "shard"), None, None),
        P(("replica", "shard"), None, None),
        P(("replica", "shard"), None, None),
    )
    return jax.shard_map(
        on_device,
        mesh=mesh,
        in_specs=placed,
        out_specs=(
            P(("replica", "shard"), None, None),
            P(("replica", "shard"), None, None),
            P("shard", "replica"),
        ),
        check_vma=False,
    )
```

profile of v0, /device:TPU:1, one launch (start us, length us, event | category | flops | bytes accessed | tf_op | source)
XLA Modules:
  0.0 320.5 jit_solution(140709671748204440)
XLA Ops:
  7.2 0.0 copy-start
  7.2 0.0 all-reduce.4.cloned.1.call-start
  7.2 4.6 %reshape.25 = bf16[64,8,4,512]{3,2,1,0:T(4,128)(2,1)} reshape(bf16[1,512,2048]{2,1,0:T(8,128)(2,1)} %param.7) | data formatting | bytes 4194304 | tf_op jit(solution)/shard_map/reshape | solution.py:28
  11.8 0.0 all-reduce.4.cloned.1.call-update
  11.8 0.0 copy-start.2
  11.8 0.0 copy-start.3
  11.8 67.7 %all-reduce.4.cloned.1.call-done = bf16[64,8,4,512]{3,2,1,0:T(4,128)(2,1)} async-done(((bf16[64,8,4,512]{3,2,1,0:T(4,128)(2,1)}), bf16[64,8,4,512]{3,2,1,0:T(4,128)(2,1)}) %all-reduce.4.cloned.1.call-update) | async-done | bytes 2097168 | tf_op jit(solution)/shard_map/psum | solution.py:27
  79.6 10.9 %all-to-all-start = ((bf16[64,8,4,512]{3,2,1,0:T(4,128)(2,1)}), bf16[64,8,4,512]{3,2,1,0:T(4,128)(2,1)}, u32[]{:S(2)}, u32[]{:S(2)}) async-start(bf16[64,8,4,512]{3,2,1,0:T(4,128)(2,1)} %all-reduce.4.cloned.1.call-done), calls=%async_computation | async-start | bytes 4194304 | tf_op jit(solution)/shard_map/all_to_all | solution.py:29
  90.5 0.0 copy-done.2
  90.5 0.0 copy-done.3
  90.5 0.4 convolution_convert_fusion.2
  90.9 19.0 %reshape.24 = bf16[4,64,2,64,4]{4,3,2,1,0:T(8,128)(2,1)} reshape(bf16[512,256]{1,0:T(8,128)(2,1)S(1)} %convolution_convert_fusion.2) | data formatting | bytes 524288 | tf_op jit(solution)/shard_map/reshape | solution.py:25
  109.9 1.8 constant_dynamic-slice_fusion.1
  111.7 1.2 copy.30
  113.0 28.6 %all-to-all-done = bf16[64,8,4,512]{3,2,1,0:T(4,128)(2,1)} async-done(((bf16[64,8,4,512]{3,2,1,0:T(4,128)(2,1)}), bf16[64,8,4,512]{3,2,1,0:T(4,128)(2,1)}, u32[]{:S(2)}, u32[]{:S(2)}) %all-to-all-start) | async-done | bytes 2097184 | tf_op jit(solution)/shard_map/all_to_all | solution.py:29
  141.6 4.1 %bitcast_convert_fusion.1 = bf16[64,2,8,512]{3,0,2,1:T(8,128)(2,1)S(1)} fusion(bf16[64,8,4,512]{3,2,1,0:T(4,128)(2,1)} %all-to-all-done, bf16[1,64,2,64,4]{3,1,4,2,0:T(8,128)(2,1)S(1)} %copy.30), kind=kOutput, calls=%fused_computation.1 | convolution fusion | flops 268959744 | bytes 3211264 | tf_op jit(solution)/shard_map/skij,iajc->skac/dot_general | solution.py:30
  145.7 0.6 copy.32
  146.3 34.2 %all_to_all.34 = bf16[64,2,8,512]{3,2,1,0:T(8,128)(2,1)S(1)} all-to-all(bf16[64,2,8,512]{3,2,1,0:T(8,128)(2,1)S(1)} %copy.32), channel_id=1, replica_groups=mesh['replica'=4,'shard'=64] {'shard'}, dimensions={0} | all-to-all | bytes 2097152 | tf_op jit(solution)/shard_map/all_to_all | solution.py:33
  180.5 0.0 copy-done
  180.5 2.5 fusion.6
  182.9 2.0 copy.35
  185.0 6.2 %all-to-all-start.2 = ((bf16[2,64,8,512]{3,0,2,1:T(2,128)(2,1)}), bf16[2,64,8,512]{3,0,2,1:T(2,128)(2,1)S(1)}, u32[]{:S(2)}, u32[]{:S(2)}) async-start(bf16[2,64,8,512]{3,0,2,1:T(2,128)(2,1)} %copy.35), calls=%async_computation.2 | async-start | bytes 2097152 | tf_op jit(solution)/shard_map/all_to_all | solution.py:45
  191.2 0.2 all-reduce.6.cloned.1.call-start
  191.4 3.2 %fusion.24 = bf16[64,2,64,4,1]{3,2,1,0,4:T(8,128)(2,1)} fusion(bf16[4,64,2,64,4]{4,3,2,1,0:T(8,128)(2,1)} %reshape.24, s32[]{:T(128)S(6)} %select_n.16), kind=kLoop, calls=%fused_computation.35 | loop fusion | bytes 131076 | tf_op jit(solution)/shard_map/jit(dynamic_index_in_dim)/squeeze | solution.py:26
  194.7 2.3 copy.43
  197.0 22.8 %all-to-all-done.2 = bf16[2,64,8,512]{3,0,2,1:T(2,128)(2,1)S(1)} async-done(((bf16[2,64,8,512]{3,0,2,1:T(2,128)(2,1)}), bf16[2,64,8,512]{3,0,2,1:T(2,128)(2,1)S(1)}, u32[]{:S(2)}, u32[]{:S(2)}) %all-to-all-start.2) | async-done | bytes 1048608 | tf_op jit(solution)/shard_map/all_to_all | solution.py:45
  219.8 0.0 copy-start.4
  219.8 3.0 fusion.3
  222.7 0.0 all-reduce.6.cloned.1.call-update
  222.8 0.0 copy-done.4
  222.8 0.6 dynamic-slice
  223.4 58.7 %all-reduce.6.cloned.1.call-done = bf16[64,8,4,512]{3,0,2,1:T(8,128)(2,1)} async-done(((bf16[64,8,4,512]{3,0,2,1:T(8,128)(2,1)}), bf16[64,8,4,512]{3,0,2,1:T(8,128)(2,1)}) %all-reduce.6.cloned.1.call-update) | async-done | bytes 2097168
  282.0 1.7 constant_dynamic-slice_fusion
  283.8 1.1 copy.38
  284.9 10.7 %all-to-all-start.3 = ((bf16[64,8,1,512]{3,1,2,0:T(8,128)(2,1)}), bf16[64,8,1,512]{3,1,2,0:T(8,128)(2,1)S(1)}, u32[]{:S(2)}, u32[]{:S(2)}) async-start(bf16[64,8,1,512]{3,1,2,0:T(8,128)(2,1)} %copy.38), calls=%async_computation.3 | async-start | bytes 1048576 | tf_op jit(solution)/shard_map/all_to_all | solution.py:50
  295.6 0.0 copy-start.1
  295.6 3.8 %multiply_add_fusion = f32[2,512,512]{2,1,0:T(8,128)} fusion(f32[2,512,512]{2,1,0:T(8,128)} %param.11, bf16[64,2,8,512]{3,2,1,0:T(8,128)(2,1)S(1)} %all_to_all.34), kind=kOutput, calls=%fused_computation.5 | convolution fusion | flops 537919488 | bytes 5242880 | tf_op jit(solution)/shard_map/kba,kbc->kac/dot_general | solution.py:35
  299.4 0.0 copy-done.1
  299.4 2.1 multiply_add_fusion.1
  301.5 11.4 %all-to-all-done.3 = bf16[64,8,1,512]{3,1,2,0:T(8,128)(2,1)S(1)} async-done(((bf16[64,8,1,512]{3,1,2,0:T(8,128)(2,1)}), bf16[64,8,1,512]{3,1,2,0:T(8,128)(2,1)S(1)}, u32[]{:S(2)}, u32[]{:S(2)}) %all-to-all-start.3) | async-done | bytes 524320 | tf_op jit(solution)/shard_map/all_to_all | solution.py:50
  312.9 0.8 copy.76
  (1 shorter events, 0.0 us)
Async XLA Ops:
  7.2 173.3 %copy-start = (bf16[2,512,512]{2,1,0:T(8,128)(2,1)S(1)}, bf16[2,512,512]{2,1,0:T(8,128)(2,1)}, u32[]{:S(2)}) copy-start(bf16[2,512,512]{2,1,0:T(8,128)(2,1)} %param.12) | copy-start | bytes 3145732
  7.2 72.4 %all-reduce.4.cloned.1.call-start = ((), (), s32[]{:S(2)}) async-start(), calls=%async_computation.4 | async-start | bytes 4194304 | tf_op jit(solution)/shard_map/psum | solution.py:27
  11.8 78.6 %copy-start.2 = (s32[256,2]{0,1:T(2,128)S(1)}, s32[256,2]{0,1:T(2,128)}, u32[]{:S(2)}) copy-start(s32[256,2]{0,1:T(2,128)} %param.9) | copy-start | bytes 6148
  11.8 78.7 %copy-start.3 = (s32[256]{0:T(256)S(1)}, s32[256]{0:T(256)}, u32[]{:S(2)}) copy-start(s32[256]{0:T(256)} %param.8) | copy-start | bytes 3076
  79.6 62.0 %all-to-all-start = ((bf16[64,8,4,512]{3,2,1,0:T(4,128)(2,1)}), bf16[64,8,4,512]{3,2,1,0:T(4,128)(2,1)}, u32[]{:S(2)}, u32[]{:S(2)}) async-start(bf16[64,8,4,512]{3,2,1,0:T(4,128)(2,1)} %all-reduce.4.cloned.1.call-done), calls=%async_computation | async-start | bytes 4194304 | tf_op jit(solution)/shard_map/all_to_all | solution.py:29
  185.0 34.8 %all-to-all-start.2 = ((bf16[2,64,8,512]{3,0,2,1:T(2,128)(2,1)}), bf16[2,64,8,512]{3,0,2,1:T(2,128)(2,1)S(1)}, u32[]{:S(2)}, u32[]{:S(2)}) async-start(bf16[2,64,8,512]{3,0,2,1:T(2,128)(2,1)} %copy.35), calls=%async_computation.2 | async-start | bytes 2097152 | tf_op jit(solution)/shard_map/all_to_all | solution.py:45
  191.2 90.8 %all-reduce.6.cloned.1.call-start = ((), (), s32[]{:S(2)}) async-start(), calls=%async_computation.5 | async-start | bytes 4194304
  219.8 3.0 copy-start.4
  284.9 28.0 %all-to-all-start.3 = ((bf16[64,8,1,512]{3,1,2,0:T(8,128)(2,1)}), bf16[64,8,1,512]{3,1,2,0:T(8,128)(2,1)S(1)}, u32[]{:S(2)}, u32[]{:S(2)}) async-start(bf16[64,8,1,512]{3,1,2,0:T(8,128)(2,1)} %copy.38), calls=%async_computation.3 | async-start | bytes 1048576 | tf_op jit(solution)/shard_map/all_to_all | solution.py:50
  295.6 3.8 %copy-start.1 = (f32[2,512,512]{2,1,0:T(8,128)S(1)}, f32[2,512,512]{2,1,0:T(8,128)}, u32[]{:S(2)}) copy-start(f32[2,512,512]{2,1,0:T(8,128)} %param.10) | copy-start | bytes 6291460
Sparse Core Ops, SparseCore 0:
  11.9 67.5 all-reduce.3
  222.9 59.1 all-reduce.5
where the time goes:
time: 321 us
  waiting for transfers between devices  189 us (59%)
  local copies, waits for them, and re-layouts  39 us (12%)
  blocking collectives  34.2 us (11%)
  starting transfers between devices  28 us (9%)
  matrix products  15.9 us (5%)
  between operations  14.2 us (4%)
    psum x1, waiting for transfers between devices, on_device(): lax.psum(grads[0].astype(jnp.float32).astype(jnp.bfloat16), 'replica')  67.7 us
    unnamed x3, waiting for transfers between devices  58.7 us
    all_to_all x1, blocking collectives, on_device(): lax.all_to_all(outgoing, 'shard', split_axis=0, concat_axis=2, tiled=True)  34.2 us
    all_to_all x1, waiting for transfers between devices, on_device(): lax.all_to_all(parts, 'shard', split_axis=0, concat_axis=0, tiled=True)  28.6 us
    all_to_all x1, waiting for transfers between devices, on_device(): lax.all_to_all(pieces, 'shard', split_axis=1, concat_axis=1, tiled=True)  22.8 us
    reshape x1, local copies, waits for them, and re-layouts, on_device(): select = select.reshape(replicas, shards, slots, shards, ncols)  19 us
    all_to_all x1, waiting for transfers between devices, on_device(): lax.all_to_all(filled, 'shard', split_axis=0, concat_axis=1, tiled=True)  11.4 us
    all_to_all x1, starting transfers between devices, on_device(): lax.all_to_all(parts, 'shard', split_axis=0, concat_axis=0, tiled=True)  10.9 us
  transfers between devices with their start and end apart: 5, of which 5 were waited for; matrix products, arithmetic and copies ran while one was open for 11% of the time, Pallas kernels for 0%

commit v1 on v0

v1 whole, which is shorter than its diff:
```python
import functools

import jax
import jax.numpy as jnp
from jax import lax
from jax.experimental import pallas as pl
from jax.experimental.pallas import tpu as pltpu
from jax.sharding import PartitionSpec as P

ROWS = 8
LANES = 128
UNROLL = 8
VMEM_LIMIT = 48 * 1024 * 1024


def combine_kernel(ncols, me_ref, own_ref, *refs):
    out_ref = refs[-1]
    right_plain, right_sum, left_plain, left_sum = refs[:-1]
    half = right_plain.shape[0]
    across = out_ref.shape[1]
    for side, (first, second) in enumerate(((right_sum, left_plain), (right_plain, left_sum))):
        rows = pl.ds(side * half, half)
        total = (
            own_ref[0, rows, :].astype(jnp.float32)
            + first[...].astype(jnp.float32)
            + second[...].astype(jnp.float32)
        ).astype(out_ref.dtype)
        groups = half // ROWS
        for block in range(ncols):
            for tile in range(across):
                lane = (block * across + tile) * LANES
                piece = total[:, lane : lane + LANES].reshape(groups, ROWS, LANES)
                out_ref[side * groups : (side + 1) * groups, tile, block] = piece


def combine(me, grads, right_plain, right_sum, left_plain, left_sum, ncols):
    replicas, rows, cols = grads.shape
    across = cols // ncols // LANES
    whole = lambda array: pl.BlockSpec(array.shape, lambda step, me_ref: (0,) * array.ndim)
    parts = (right_plain, right_sum, left_plain, left_sum)
    shape = (rows // ROWS, across, ncols, ROWS, LANES)
    return pl.pallas_call(
        functools.partial(combine_kernel, ncols),
        out_shape=jax.ShapeDtypeStruct(shape, grads.dtype),
        grid_spec=pltpu.PrefetchScalarGridSpec(
            num_scalar_prefetch=1,
            grid=(1,),
            in_specs=[
                pl.BlockSpec((1, rows, cols), lambda step, me_ref: (me_ref[0], 0, 0)),
                *[whole(part) for part in parts],
            ],
            out_specs=pl.BlockSpec(shape, lambda step, me_ref: (0,) * len(shape)),
        ),
        compiler_params=pltpu.CompilerParams(vmem_limit_bytes=VMEM_LIMIT),
        name="combine",
    )(me, grads, *parts)


def place_kernel(zero, source_ref, target_ref, in_ref, out_ref):
    if zero:
        out_ref[...] = jnp.zeros_like(out_ref)

    def step(group, carry):
        for offset in range(UNROLL):
            index = group * UNROLL + offset
            out_ref[target_ref[index]] = in_ref[source_ref[index]]
        return carry

    lax.fori_loop(0, source_ref.shape[0] // UNROLL, step, 0)


def place(source, target, tiles, count, zero):
    shape = (count,) + tiles.shape[1:]
    return pl.pallas_call(
        functools.partial(place_kernel, zero),
        out_shape=jax.ShapeDtypeStruct(shape, tiles.dtype),
        grid_spec=pltpu.PrefetchScalarGridSpec(
            num_scalar_prefetch=2,
            grid=(1,),
            in_specs=[pl.BlockSpec(tiles.shape, lambda step, *refs: (0, 0, 0))],
            out_specs=pl.BlockSpec(shape, lambda step, *refs: (0, 0, 0)),
        ),
        compiler_params=pltpu.CompilerParams(vmem_limit_bytes=VMEM_LIMIT),
        name="place",
    )(source, target, tiles)


def assemble(tiles_ref):
    groups, across = tiles_ref.shape[:2]
    columns = [tiles_ref[:, tile, 0].reshape(groups * ROWS, LANES) for tile in range(across)]
    return jnp.concatenate(columns, axis=1)


def steer_kernel(tiles_ref, left_ref, right_ref, out_ref):
    block = assemble(tiles_ref)
    right_side = jnp.dot(block, right_ref[0], preferred_element_type=jnp.float32).astype(
        out_ref.dtype
    )
    steer = jnp.dot(left_ref[0], right_side, preferred_element_type=jnp.float32).astype(
        out_ref.dtype
    )
    groups, across = out_ref.shape[:2]
    for tile in range(across):
        out_ref[:, tile, 0] = steer[:, tile * LANES : (tile + 1) * LANES].reshape(
            groups, ROWS, LANES
        )


def gram_kernel(tiles_ref, left_ref, right_ref, new_left_ref, new_right_ref):
    block = assemble(tiles_ref)
    width = block.shape[0]
    gram_left = lax.dot_general(
        block, block, (((1,), (1,)), ((), ())), preferred_element_type=jnp.float32
    )
    new_left_ref[0] = left_ref[0] + gram_left / width
    gram_right = lax.dot_general(
        block, block, (((0,), (0,)), ((), ())), preferred_element_type=jnp.float32
    )
    new_right_ref[0] = right_ref[0] + gram_right / width


def slot_specs(tiles, square):
    groups, across = tiles.shape[:2]
    return (
        pl.BlockSpec((groups, across, 1, ROWS, LANES), lambda slot: (0, 0, slot, 0, 0)),
        pl.BlockSpec((1, square, square), lambda slot: (slot, 0, 0)),
    )


def steer_slots(tiles, root_left, root_right):
    slots, width = root_left.shape[:2]
    tiled, square = slot_specs(tiles, width)
    return pl.pallas_call(
        steer_kernel,
        out_shape=jax.ShapeDtypeStruct(tiles.shape, tiles.dtype),
        grid=(slots,),
        in_specs=[tiled, square, square],
        out_specs=tiled,
        compiler_params=pltpu.CompilerParams(vmem_limit_bytes=VMEM_LIMIT),
        cost_estimate=pl.CostEstimate(
            flops=4 * slots * width**3, bytes_accessed=8 * slots * width**2, transcendentals=0
        ),
        name="steer",
    )(tiles, root_left, root_right)


def gram_slots(tiles, stat_left, stat_right):
    slots, width = stat_left.shape[:2]
    tiled, square = slot_specs(tiles, width)
    return pl.pallas_call(
        gram_kernel,
        out_shape=[jax.ShapeDtypeStruct(stat.shape, stat.dtype) for stat in (stat_left, stat_right)],
        grid=(slots,),
        in_specs=[tiled, square, square],
        out_specs=[square, square],
        compiler_params=pltpu.CompilerParams(vmem_limit_bytes=VMEM_LIMIT),
        cost_estimate=pl.CostEstimate(
            flops=4 * slots * width**3, bytes_accessed=18 * slots * width**2, transcendentals=0
        ),
        name="gram",
    )(tiles, stat_left, stat_right)


def reduce_rows(grads, replicas, ncols):
    rows, cols = grads.shape[1] // replicas, grads.shape[2]
    parts = grads.reshape(replicas, 2, rows // 2, cols)
    me = lax.axis_index("replica")
    rightward = [(i, (i + 1) % replicas) for i in range(replicas)]
    leftward = [(i, (i - 1) % replicas) for i in range(replicas)]

    def part(shift, side):
        index = lax.rem(me + shift, replicas)
        return lax.dynamic_slice(parts, (index, side, 0, 0), (1, 1, rows // 2, cols))[0, 0]

    from_left = lax.ppermute(part(2, 0), "replica", rightward)
    from_right = lax.ppermute(part(2, 1), "replica", leftward)
    right_plain = lax.ppermute(part(1, 1), "replica", rightward)
    left_plain = lax.ppermute(part(3, 0), "replica", leftward)

    def add(first, second):
        return (first.astype(jnp.float32) + second.astype(jnp.float32)).astype(grads.dtype)

    right_sum = lax.ppermute(add(part(1, 0), from_left), "replica", rightward)
    left_sum = lax.ppermute(add(part(3, 1), from_right), "replica", leftward)
    return combine(
        jnp.reshape(me, (1,)).astype(jnp.int32),
        grads.reshape(replicas, rows, cols),
        right_plain,
        right_sum,
        left_plain,
        left_sum,
        ncols,
    )


def on_device(grads, block_owner, block_offsets, stat_left, stat_right, root_left, root_right):
    shards = lax.axis_size("shard")
    replicas = lax.axis_size("replica")
    devices = replicas * shards
    slots, width = stat_left.shape[:2]
    ncols = grads.shape[2] // width
    blocks = block_owner.shape[0]
    across = width // LANES
    groups = width // ROWS
    row = block_offsets[:, 0] // width
    col = block_offsets[:, 1] // width

    summed = reduce_rows(grads, replicas, ncols)
    spread = lax.all_to_all(
        summed.reshape(shards, ncols, ROWS, LANES), "shard", split_axis=0, concat_axis=0, tiled=True
    )
    by_slot = place(
        row * ncols + col, block_owner, spread.reshape(blocks, ROWS, LANES), devices * slots, True
    )
    everyone = ("replica", "shard")
    owned = lax.all_to_all(
        by_slot.reshape(devices, slots, ROWS, LANES),
        everyone,
        split_axis=0,
        concat_axis=0,
        tiled=True,
    ).reshape(groups, across, slots, ROWS, LANES)
    steer = steer_slots(owned, root_left, root_right)
    new_left, new_right = gram_slots(owned, stat_left, stat_right)
    returned = lax.all_to_all(
        steer.reshape(devices, slots, ROWS, LANES),
        everyone,
        split_axis=0,
        concat_axis=0,
        tiled=True,
    )
    by_place = place(
        block_owner,
        col * shards + row,
        returned.reshape(devices * slots, ROWS, LANES),
        blocks,
        False,
    )
    home = lax.all_to_all(by_place, everyone, split_axis=0, concat_axis=0, tiled=True)
    direction = (
        home.reshape(groups, across, ROWS, LANES).transpose(0, 2, 1, 3).reshape(width, width)
    )
    return (new_left, new_right, direction)


def solution(mesh):
    placed = (
        P("replica", "shard", None),
        P(),
        P(),
        P(("replica", "shard"), None, None),
        P(("replica", "shard"), None, None),
        P(("replica", "shard"), None, None),
        P(("replica", "shard"), None, None),
    )
    return jax.shard_map(
        on_device,
        mesh=mesh,
        in_specs=placed,
        out_specs=(
            P(("replica", "shard"), None, None),
            P(("replica", "shard"), None, None),
            P("shard", "replica"),
        ),
        check_vma=False,
    )
```

time: 321 us -> 166 us (0.52)
  waiting for transfers between devices: 189 us -> 47.1 us
  blocking collectives: 34.2 us -> 75.5 us
  local copies, waits for them, and re-layouts: 39 us -> 5.71 us
  matrix products: 15.9 us -> 0 us
  between operations: 14.2 us -> 0.8 us
  Pallas kernels: 0 us -> 8.26 us
    psum x1 -> x0, waiting for transfers between devices: 67.7 us -> none  [on_device(): lax.psum(grads[0].astype(jnp.float32).astype(jnp.bfloat16), 'replica')]
    unnamed x3 -> x0, waiting for transfers between devices: 58.7 us -> none
    all_to_all x1 -> x2, blocking collectives: 34.2 us -> 75.5 us  [the longest x1 38.6 us: on_device(): lax.all_to_all(by_slot.reshape(devices, slots, ROWS, LANES), everyone, sp...]
    all_to_all x3 -> x2, waiting for transfers between devices: 62.8 us -> 32.1 us  [the longest x1 17.2 us: on_device(): lax.all_to_all(summed.reshape(shards, ncols, ROWS, LANES), 'shard', split...]
    reshape x3 -> x0, local copies, waits for them, and re-layouts: 25.6 us -> none  [the longest x1 19 us: on_device(): select = select.reshape(replicas, shards, slots, shards, ncols)]
    dot_general x6 -> x0, matrix products: 15.9 us -> none  [the longest x1 4.08 us: on_device(): jnp.einsum('skij,iajc->skac', here, arrived, preferred_element_type=jnp.f...]
    ppermute x0 -> x6, waiting for transfers between devices: none -> 14.9 us  [the longest x1 3.09 us: reduce_rows(): from_left = lax.ppermute(part(2, 0), 'replica', rightward)]
    pallas_call x0 -> x5, Pallas kernels: none -> 8.26 us  [the longest x1 2.76 us: gram_slots(): pl.pallas_call(gram_kernel, out_shape=[jax.ShapeDtypeStruct(stat.shape, s...]
  transfers between devices with their start and end apart: 5 -> 8, of which waited for: 5 -> 8; matrix products, arithmetic and copies ran while one was open for 11% -> 0% of each run, Pallas kernels for 0% -> 2%
where the time goes in v1:
time: 166 us; the launch traced here: 165 us
  blocking collectives  75.5 us (45%)
  waiting for transfers between devices  47.1 us (28%)
  starting transfers between devices  28 us (17%)
  Pallas kernels  8.26 us (5%)
  local copies, waits for them, and re-layouts  5.71 us (3%)
    all_to_all x1, blocking collectives, on_device(): lax.all_to_all(by_slot.reshape(devices, slots, ROWS, LANES), everyone, sp...  38.6 us
    all_to_all x1, blocking collectives, on_device(): lax.all_to_all(steer.reshape(devices, slots, ROWS, LANES), everyone, spli...  36.9 us
    all_to_all x1, waiting for transfers between devices, on_device(): lax.all_to_all(summed.reshape(shards, ncols, ROWS, LANES), 'shard', split...  17.2 us
    all_to_all x1, waiting for transfers between devices, on_device(): lax.all_to_all(by_place, everyone, split_axis=0, concat_axis=0, tiled=True)  14.9 us
    all_to_all x1, starting transfers between devices, on_device(): lax.all_to_all(summed.reshape(shards, ncols, ROWS, LANES), 'shard', split...  13.5 us
    all_to_all x1, starting transfers between devices, on_device(): lax.all_to_all(by_place, everyone, split_axis=0, concat_axis=0, tiled=True)  6.83 us
    unnamed x17, local copies, waits for them, and re-layouts  4.27 us
    ppermute x1, starting transfers between devices, reduce_rows(): from_right = lax.ppermute(part(2, 1), 'replica', leftward)  3.39 us
  transfers between devices with their start and end apart: 8, of which 8 were waited for; matrix products, arithmetic and copies ran while one was open for 0% of the time, Pallas kernels for 2%

profile of v1, /device:TPU:1, one launch (start us, length us, event | category | flops | bytes accessed | tf_op | source)
XLA Modules:
  0.0 165.5 jit_solution(2205524605886819741)
XLA Ops:
  0.6 0.0 copy-start
  0.7 1.4 dynamic-slice_bitcast_fusion
  2.1 3.4 %collective-permute-start.4 = (bf16[64,2048]{1,0:T(8,128)(2,1)S(1)}, bf16[64,2048]{1,0:T(8,128)(2,1)S(1)}, u32[]{:S(2)}, u32[]{:S(2)}) collective-permute-start(bf16[64,2048]{1,0:T(8,128)(2,1)S(1)} %get-tuple-element.12), channel_id=1, source_target_pairs={{0,192},{64,0},{128,64},{192,128},{1,193},{65,1},{129,65},{193,129... | collective-permute-start | bytes 786440 | tf_op jit(solution)/shard_map/ppermute | solution.py:176
  5.5 0.0 collective-permute-start.1
  5.5 2.7 %collective-permute-start.3 = (bf16[64,2048]{1,0:T(8,128)(2,1)S(1)}, bf16[64,2048]{1,0:T(8,128)(2,1)S(1)}, u32[]{:S(2)}, u32[]{:S(2)}) collective-permute-start(bf16[64,2048]{1,0:T(8,128)(2,1)S(1)} %get-tuple-element.13), channel_id=1, source_target_pairs={{0,192},{64,0},{128,64},{192,128},{1,193},{65,1},{129,65},{193,129... | collective-permute-start | bytes 786440 | tf_op jit(solution)/shard_map/ppermute | solution.py:178
  8.2 0.0 collective-permute-start
  8.2 2.3 %collective-permute-done.4 = bf16[64,2048]{1,0:T(8,128)(2,1)S(1)} collective-permute-done((bf16[64,2048]{1,0:T(8,128)(2,1)S(1)}, bf16[64,2048]{1,0:T(8,128)(2,1)S(1)}, u32[]{:S(2)}, u32[]{:S(2)}) %collective-permute-start.4) | collective-permute-done | bytes 262176 | tf_op jit(solution)/shard_map/ppermute | solution.py:176
  10.5 3.1 %collective-permute-done.1 = bf16[64,2048]{1,0:T(8,128)(2,1)S(1)} collective-permute-done((bf16[64,2048]{1,0:T(8,128)(2,1)S(1)}, bf16[64,2048]{1,0:T(8,128)(2,1)S(1)}, u32[]{:S(2)}, u32[]{:S(2)}) %collective-permute-start.1) | collective-permute-done | bytes 262176 | tf_op jit(solution)/shard_map/ppermute | solution.py:175
  13.6 0.0 copy-done
  13.6 0.1 fusion
  13.7 0.4 collective-permute-start.5
  14.1 1.1 collective-permute-start.2
  15.2 0.8 collective-permute-done.3.refs_2_
  16.1 3.1 %collective-permute-done.refs_0_ = bf16[64,2048]{1,0:T(8,128)(2,1)S(1)} collective-permute-done((bf16[64,2048]{1,0:T(8,128)(2,1)S(1)}, bf16[64,2048]{1,0:T(8,128)(2,1)S(1)}, u32[]{:S(2)}, u32[]{:S(2)}) %collective-permute-start) | collective-permute-done | bytes 262176 | tf_op jit(solution)/shard_map/ppermute | solution.py:177
  19.2 2.5 %collective-permute-done.5.refs_3_ = bf16[64,2048]{1,0:T(8,128)(2,1)S(1)} collective-permute-done((bf16[64,2048]{1,0:T(8,128)(2,1)S(1)}, bf16[64,2048]{1,0:T(8,128)(2,1)S(1)}, u32[]{:S(2)}, u32[]{:S(2)}) %collective-permute-start.5) | collective-permute-done | bytes 262176 | tf_op jit(solution)/shard_map/ppermute | solution.py:184
  21.7 3.1 %collective-permute-done.2.refs_1_ = bf16[64,2048]{1,0:T(8,128)(2,1)S(1)} collective-permute-done((bf16[64,2048]{1,0:T(8,128)(2,1)S(1)}, bf16[64,2048]{1,0:T(8,128)(2,1)S(1)}, u32[]{:S(2)}, u32[]{:S(2)}) %collective-permute-start.2) | collective-permute-done | bytes 262176 | tf_op jit(solution)/shard_map/ppermute | solution.py:183
  24.8 0.0 copy-start.7
  24.8 0.0 copy-start.6
  24.8 1.0 combine.1
  25.8 13.5 %all-to-all-start = ((bf16[64,4,8,128]{3,2,1,0:T(8,128)(2,1)}), bf16[64,4,8,128]{3,2,1,0:T(8,128)(2,1)S(1)}, u32[]{:S(2)}, u32[]{:S(2)}) async-start(bf16[64,4,8,128]{3,2,1,0:T(8,128)(2,1)} %bitcast.11), calls=%async_computation | async-start | bytes 1048576 | tf_op jit(solution)/shard_map/all_to_all | solution.py:209
  39.3 0.0 copy-done.7
  39.3 0.0 copy-start.4
  39.4 0.0 copy-start.5
  39.4 17.2 %all-to-all-done = bf16[64,4,8,128]{3,2,1,0:T(8,128)(2,1)S(1)} async-done(((bf16[64,4,8,128]{3,2,1,0:T(8,128)(2,1)}), bf16[64,4,8,128]{3,2,1,0:T(8,128)(2,1)S(1)}, u32[]{:S(2)}, u32[]{:S(2)}) %all-to-all-start) | async-done | bytes 524320 | tf_op jit(solution)/shard_map/all_to_all | solution.py:209
  56.7 0.0 copy-done.6
  56.7 1.3 place.2
  58.0 38.6 %all_to_all.20 = bf16[256,2,8,128]{3,2,1,0:T(8,128)(2,1)S(1)} all-to-all(bf16[256,2,8,128]{3,2,1,0:T(8,128)(2,1)S(1)} %bitcast.36), channel_id=1, replica_groups=mesh['replica'=4,'shard'=64] {'replica','shard'}, dimensions={0} | all-to-all | bytes 2097152 | tf_op jit(solution)/shard_map/all_to_all | solution.py:216
  96.6 0.0 copy-done.4
  96.6 0.0 copy-done.5
  96.6 2.0 %steer.1 = bf16[64,4,2,8,128]{4,3,2,1,0:T(8,128)(2,1)S(1)} custom-call(bf16[64,4,2,8,128]{4,3,2,1,0:T(8,128)(2,1)S(1)} %bitcast.30, bf16[2,512,512]{2,1,0:T(8,128)(2,1)S(1)} %copy-done.4, bf16[2,512,512]{2,1,0:T(8,128)(2,1)S(1)} %copy-done.5), custom_call_target="tpu_custom_call" | custom-call | flops 1073741824 | bytes 4194304 | tf_op jit(solution)/shard_map/steer/pallas_call | solution.py:133
  98.6 0.0 copy-start.1
  98.6 36.9 %all_to_all.21 = bf16[256,2,8,128]{3,2,1,0:T(8,128)(2,1)S(1)} all-to-all(bf16[256,2,8,128]{3,2,1,0:T(8,128)(2,1)S(1)} %bitcast.37), channel_id=1, replica_groups=mesh['replica'=4,'shard'=64] {'replica','shard'}, dimensions={0} | all-to-all | bytes 2097152 | tf_op jit(solution)/shard_map/all_to_all | solution.py:225
  135.5 1.2 place.3
  136.7 0.0 copy-start.3
  136.7 0.8 copy-done.3
  137.5 6.8 %all-to-all-start.3 = ((bf16[256,8,128]{2,1,0:T(8,128)(2,1)}), bf16[256,8,128]{2,1,0:T(8,128)(2,1)}, u32[]{:S(2)}, u32[]{:S(2)}) async-start(bf16[256,8,128]{2,1,0:T(8,128)(2,1)} %copy-done.3), calls=%async_computation.3 | async-start | bytes 1048576 | tf_op jit(solution)/shard_map/all_to_all | solution.py:239
  144.3 0.0 copy-done.1
  144.4 0.0 copy-start.2
  144.4 1.6 copy-done.2
  146.0 2.8 %gram.1 = (f32[2,512,512]{2,1,0:T(8,128)}, f32[2,512,512]{2,1,0:T(8,128)}) custom-call(bf16[64,4,2,8,128]{4,3,2,1,0:T(8,128)(2,1)S(1)} %bitcast.31, f32[2,512,512]{2,1,0:T(8,128)S(1)} %copy-done.1, f32[2,512,512]{2,1,0:T(8,128)S(1)} %copy-done.2), custom_call_target="tpu_custom_call" | custom-call | flops 1073741824 | bytes 9437184 | tf_op jit(solution)/shard_map/gram/pallas_call | solution.py:150
  148.7 14.9 %all-to-all-done.3 = bf16[256,8,128]{2,1,0:T(8,128)(2,1)} async-done(((bf16[256,8,128]{2,1,0:T(8,128)(2,1)}), bf16[256,8,128]{2,1,0:T(8,128)(2,1)}, u32[]{:S(2)}, u32[]{:S(2)}) %all-to-all-start.3) | async-done | bytes 524320 | tf_op jit(solution)/shard_map/all_to_all | solution.py:239
  163.6 1.9 %copy.11 = bf16[512,512]{1,0:T(8,128)(2,1)} copy(bf16[512,512]{1,0:T(8,128)(2,1)} %bitcast.19) | data formatting | bytes 1048576
  (3 shorter events, 0.0 us)
Async XLA Ops:
  0.6 12.9 %copy-start = (bf16[1,512,2048]{2,1,0:T(8,128)(2,1)S(1)}, bf16[1,512,2048]{2,1,0:T(8,128)(2,1)}, u32[]{:S(2)}) copy-start(bf16[1,512,2048]{2,1,0:T(8,128)(2,1)} %param.7) | copy-start | bytes 6291460
  2.1 8.4 %collective-permute-start.4 = (bf16[64,2048]{1,0:T(8,128)(2,1)S(1)}, bf16[64,2048]{1,0:T(8,128)(2,1)S(1)}, u32[]{:S(2)}, u32[]{:S(2)}) collective-permute-start(bf16[64,2048]{1,0:T(8,128)(2,1)S(1)} %get-tuple-element.12), channel_id=1, source_target_pairs={{0,192},{64,0},{128,64},{192,128},{1,193},{65,1},{129,65},{193,129... | collective-permute-start | bytes 786440 | tf_op jit(solution)/shard_map/ppermute | solution.py:176
  5.5 8.1 %collective-permute-start.1 = (bf16[64,2048]{1,0:T(8,128)(2,1)S(1)}, bf16[64,2048]{1,0:T(8,128)(2,1)S(1)}, u32[]{:S(2)}, u32[]{:S(2)}) collective-permute-start(bf16[64,2048]{1,0:T(8,128)(2,1)S(1)} %get-tuple-element.14), channel_id=1, source_target_pairs={{0,64},{64,128},{128,192},{192,0},{1,65},{65,129},{129,193},{193,1... | collective-permute-start | bytes 786440 | tf_op jit(solution)/shard_map/ppermute | solution.py:175
  5.5 10.6 %collective-permute-start.3 = (bf16[64,2048]{1,0:T(8,128)(2,1)S(1)}, bf16[64,2048]{1,0:T(8,128)(2,1)S(1)}, u32[]{:S(2)}, u32[]{:S(2)}) collective-permute-start(bf16[64,2048]{1,0:T(8,128)(2,1)S(1)} %get-tuple-element.13), channel_id=1, source_target_pairs={{0,192},{64,0},{128,64},{192,128},{1,193},{65,1},{129,65},{193,129... | collective-permute-start | bytes 786440 | tf_op jit(solution)/shard_map/ppermute | solution.py:178
  8.2 11.0 %collective-permute-start = (bf16[64,2048]{1,0:T(8,128)(2,1)S(1)}, bf16[64,2048]{1,0:T(8,128)(2,1)S(1)}, u32[]{:S(2)}, u32[]{:S(2)}) collective-permute-start(bf16[64,2048]{1,0:T(8,128)(2,1)S(1)} %get-tuple-element.15), channel_id=1, source_target_pairs={{0,64},{64,128},{128,192},{192,0},{1,65},{65,129},{129,193},{193,1... | collective-permute-start | bytes 786440 | tf_op jit(solution)/shard_map/ppermute | solution.py:177
  13.7 8.0 %collective-permute-start.5 = (bf16[64,2048]{1,0:T(8,128)(2,1)S(1)}, bf16[64,2048]{1,0:T(8,128)(2,1)S(1)}, u32[]{:S(2)}, u32[]{:S(2)}) collective-permute-start(bf16[64,2048]{1,0:T(8,128)(2,1)S(1)} %get-tuple-element.10), channel_id=1, source_target_pairs={{0,192},{64,0},{128,64},{192,128},{1,193},{65,1},{129,65},{193,129... | collective-permute-start | bytes 786440 | tf_op jit(solution)/shard_map/ppermute | solution.py:184
  14.1 10.7 %collective-permute-start.2 = (bf16[64,2048]{1,0:T(8,128)(2,1)S(1)}, bf16[64,2048]{1,0:T(8,128)(2,1)S(1)}, u32[]{:S(2)}, u32[]{:S(2)}) collective-permute-start(bf16[64,2048]{1,0:T(8,128)(2,1)S(1)} %get-tuple-element.11), channel_id=1, source_target_pairs={{0,64},{64,128},{128,192},{192,0},{1,65},{65,129},{129,193},{193,1... | collective-permute-start | bytes 786440 | tf_op jit(solution)/shard_map/ppermute | solution.py:183
  24.8 14.5 %copy-start.7 = (s32[256,2]{0,1:T(2,128)S(1)}, s32[256,2]{0,1:T(2,128)}, u32[]{:S(2)}) copy-start(s32[256,2]{0,1:T(2,128)} %param.9) | copy-start | bytes 6148
  24.8 31.9 %copy-start.6 = (s32[256]{0:T(256)S(1)}, s32[256]{0:T(256)}, u32[]{:S(2)}) copy-start(s32[256]{0:T(256)} %source_ref.1) | copy-start | bytes 3076
  25.8 30.8 %all-to-all-start = ((bf16[64,4,8,128]{3,2,1,0:T(8,128)(2,1)}), bf16[64,4,8,128]{3,2,1,0:T(8,128)(2,1)S(1)}, u32[]{:S(2)}, u32[]{:S(2)}) async-start(bf16[64,4,8,128]{3,2,1,0:T(8,128)(2,1)} %bitcast.11), calls=%async_computation | async-start | bytes 1048576 | tf_op jit(solution)/shard_map/all_to_all | solution.py:209
  39.3 57.3 %copy-start.4 = (bf16[2,512,512]{2,1,0:T(8,128)(2,1)S(1)}, bf16[2,512,512]{2,1,0:T(8,128)(2,1)}, u32[]{:S(2)}) copy-start(bf16[2,512,512]{2,1,0:T(8,128)(2,1)} %left_ref.3) | copy-start | bytes 3145732
  39.4 57.3 %copy-start.5 = (bf16[2,512,512]{2,1,0:T(8,128)(2,1)S(1)}, bf16[2,512,512]{2,1,0:T(8,128)(2,1)}, u32[]{:S(2)}) copy-start(bf16[2,512,512]{2,1,0:T(8,128)(2,1)} %right_ref.3) | copy-start | bytes 3145732
  98.6 45.7 %copy-start.1 = (f32[2,512,512]{2,1,0:T(8,128)S(1)}, f32[2,512,512]{2,1,0:T(8,128)}, u32[]{:S(2)}) copy-start(f32[2,512,512]{2,1,0:T(8,128)} %left_ref.2) | copy-start | bytes 6291460
  136.7 0.8 copy-start.3
  137.5 26.1 %all-to-all-start.3 = ((bf16[256,8,128]{2,1,0:T(8,128)(2,1)}), bf16[256,8,128]{2,1,0:T(8,128)(2,1)}, u32[]{:S(2)}, u32[]{:S(2)}) async-start(bf16[256,8,128]{2,1,0:T(8,128)(2,1)} %copy-done.3), calls=%async_computation.3 | async-start | bytes 1048576 | tf_op jit(solution)/shard_map/all_to_all | solution.py:239
  144.4 1.6 copy-start.2

commit v2 on v1

v2 whole, which is shorter than its diff:
```python
import functools

import jax
import jax.numpy as jnp
from jax import lax
from jax.experimental import pallas as pl
from jax.experimental.pallas import tpu as pltpu
from jax.sharding import PartitionSpec as P

ROWS = 8
LANES = 128
UNROLL = 16
PARTS = 4
VMEM_LIMIT = 16 * 1024 * 1024
GRAM_VMEM = 62 * 1024 * 1024
IN_VMEM = pl.BlockSpec(memory_space=pltpu.VMEM)
IN_SMEM = pl.BlockSpec(memory_space=pltpu.SMEM)
PARAMS = pltpu.CompilerParams(vmem_limit_bytes=VMEM_LIMIT)


def combine_kernel(ncols, me_ref, own_ref, *refs):
    out_ref = refs[-1]
    right_plain, right_sum, left_plain, left_sum = refs[:-1]
    half = right_plain.shape[0]
    across = out_ref.shape[1]
    groups = half // ROWS
    me = me_ref[0]
    for side, (first, second) in enumerate(((right_sum, left_plain), (right_plain, left_sum))):
        for block in range(ncols):
            for tile in range(across):
                lanes = pl.ds((block * across + tile) * LANES, LANES)
                total = (
                    own_ref[me, side, :, lanes].astype(jnp.float32)
                    + first[:, lanes].astype(jnp.float32)
                    + second[:, lanes].astype(jnp.float32)
                ).astype(out_ref.dtype)
                rows = pl.ds(side * groups, groups)
                out_ref[rows, tile, block] = total.reshape(groups, ROWS, LANES)


def combine(me, parts, right_plain, right_sum, left_plain, left_sum, ncols):
    half, cols = right_plain.shape
    shape = (2 * half // ROWS, cols // ncols // LANES, ncols, ROWS, LANES)
    return pl.pallas_call(
        functools.partial(combine_kernel, ncols),
        out_shape=jax.ShapeDtypeStruct(shape, parts.dtype),
        in_specs=[IN_SMEM] + [IN_VMEM] * 5,
        out_specs=IN_VMEM,
        compiler_params=PARAMS,
        name="combine",
    )(me, parts, right_plain, right_sum, left_plain, left_sum)


def place_rows(source_ref, target_ref, in_ref, out_ref, begin, count):
    def step(group, carry):
        rows = [begin + group * UNROLL + offset for offset in range(UNROLL)]
        pieces = [in_ref[source_ref[row]] for row in rows]
        for row, piece in zip(rows, pieces):
            out_ref[target_ref[row]] = piece
        return carry

    lax.fori_loop(0, count // UNROLL, step, 0)


def to_slots_kernel(source_ref, target_ref, in_ref, out_ref):
    out_ref[...] = jnp.zeros_like(out_ref)
    place_rows(source_ref, target_ref, in_ref, out_ref, 0, source_ref.shape[0])


def to_slots(source, target, tiles, count):
    return pl.pallas_call(
        to_slots_kernel,
        out_shape=jax.ShapeDtypeStruct((count,) + tiles.shape[1:], tiles.dtype),
        in_specs=[IN_SMEM, IN_SMEM, IN_VMEM],
        out_specs=IN_VMEM,
        compiler_params=PARAMS,
        name="to_slots",
    )(source, target, tiles)


def pick_kernel(index_ref, in_ref, out_ref, filled, sems):
    parts = sems.shape[0]
    count = filled.shape[0] // parts

    def move(part):
        rows = pl.ds(part * count, count)
        return pltpu.make_async_copy(filled.at[rows], out_ref.at[rows], sems.at[part])

    for part in range(parts):

        def step(group, carry):
            rows = [part * count + group * UNROLL + offset for offset in range(UNROLL)]
            pieces = [in_ref[index_ref[row]] for row in rows]
            for row, piece in zip(rows, pieces):
                filled[row] = piece
            return carry

        lax.fori_loop(0, count // UNROLL, step, 0)
        move(part).start()
    for part in range(parts):
        move(part).wait()


def pick(index, tiles):
    shape = index.shape + tiles.shape[1:]
    return pl.pallas_call(
        pick_kernel,
        out_shape=jax.ShapeDtypeStruct(shape, tiles.dtype),
        in_specs=[IN_SMEM, IN_VMEM],
        out_specs=pl.BlockSpec(memory_space=pltpu.HBM),
        scratch_shapes=[pltpu.VMEM(shape, tiles.dtype), pltpu.SemaphoreType.DMA((PARTS,))],
        compiler_params=PARAMS,
        name="pick",
    )(index, tiles)


def assemble(tiles_ref, slot):
    groups, across = tiles_ref.shape[:2]
    columns = [tiles_ref[:, tile, slot].reshape(groups * ROWS, LANES) for tile in range(across)]
    return jnp.concatenate(columns, axis=1)


def steer_kernel(tiles_ref, left_ref, right_ref, out_ref):
    groups, across, slots = out_ref.shape[:3]
    for slot in range(slots):
        block = assemble(tiles_ref, slot)
        right_side = jnp.dot(block, right_ref[slot], preferred_element_type=jnp.float32)
        right_side = right_side.astype(out_ref.dtype)
        steer = jnp.dot(left_ref[slot], right_side, preferred_element_type=jnp.float32)
        steer = steer.astype(out_ref.dtype)
        for tile in range(across):
            piece = steer[:, tile * LANES : (tile + 1) * LANES]
            out_ref[:, tile, slot] = piece.reshape(groups, ROWS, LANES)


def gram_kernel(tiles_ref, left_ref, right_ref, new_left_ref, new_right_ref, held, in_sems, out_sems):
    slots, width = left_ref.shape[:2]

    def copies(slot):
        for side, (old, new) in enumerate(((left_ref, new_left_ref), (right_ref, new_right_ref))):
            space = held.at[slot, side]
            yield (
                pltpu.make_async_copy(old.at[slot], space, in_sems.at[slot, side]),
                pltpu.make_async_copy(space, new.at[slot], out_sems.at[slot, side]),
            )

    for slot in range(slots):
        for arriving, _ in copies(slot):
            arriving.start()
    for slot in range(slots):
        block = assemble(tiles_ref, slot)
        for side, (arriving, leaving) in enumerate(copies(slot)):
            contracted = ((1 - side,), (1 - side,))
            gram = lax.dot_general(
                block, block, (contracted, ((), ())), preferred_element_type=jnp.float32
            )
            arriving.wait()
            held[slot, side] += gram / width
            leaving.start()
    for slot in range(slots):
        for _, leaving in copies(slot):
            leaving.wait()


def steer_slots(tiles, root_left, root_right):
    slots, width = root_left.shape[:2]
    return pl.pallas_call(
        steer_kernel,
        out_shape=jax.ShapeDtypeStruct(tiles.shape, tiles.dtype),
        in_specs=[IN_VMEM] * 3,
        out_specs=IN_VMEM,
        compiler_params=PARAMS,
        cost_estimate=pl.CostEstimate(
            flops=4 * slots * width**3, bytes_accessed=8 * slots * width**2, transcendentals=0
        ),
        name="steer",
    )(tiles, root_left, root_right)


def gram_slots(tiles, stat_left, stat_right):
    slots, width = stat_left.shape[:2]
    in_hbm = pl.BlockSpec(memory_space=pltpu.HBM)
    return pl.pallas_call(
        gram_kernel,
        out_shape=[jax.ShapeDtypeStruct(stat.shape, stat.dtype) for stat in (stat_left, stat_right)],
        in_specs=[IN_VMEM, in_hbm, in_hbm],
        out_specs=[in_hbm, in_hbm],
        scratch_shapes=[
            pltpu.VMEM((slots, 2, width, width), jnp.float32),
            pltpu.SemaphoreType.DMA((slots, 2)),
            pltpu.SemaphoreType.DMA((slots, 2)),
        ],
        compiler_params=pltpu.CompilerParams(vmem_limit_bytes=GRAM_VMEM),
        cost_estimate=pl.CostEstimate(
            flops=4 * slots * width**3, bytes_accessed=18 * slots * width**2, transcendentals=0
        ),
        name="gram",
    )(tiles, stat_left, stat_right)


def reduce_rows(grads, replicas, ncols):
    rows, cols = grads.shape[1] // replicas, grads.shape[2]
    parts = grads.reshape(replicas, 2, rows // 2, cols)
    me = lax.axis_index("replica")
    rightward = [(i, (i + 1) % replicas) for i in range(replicas)]
    leftward = [(i, (i - 1) % replicas) for i in range(replicas)]

    def part(shift, side):
        index = lax.rem(me + shift, replicas)
        return lax.dynamic_slice(parts, (index, side, 0, 0), (1, 1, rows // 2, cols))[0, 0]

    parts, far_right, far_left = lax.optimization_barrier((parts, part(2, 0), part(2, 1)))
    from_left = lax.ppermute(far_right, "replica", rightward)
    from_right = lax.ppermute(far_left, "replica", leftward)
    right_plain = lax.ppermute(part(1, 1), "replica", rightward)
    left_plain = lax.ppermute(part(3, 0), "replica", leftward)

    def add(first, second):
        return (first.astype(jnp.float32) + second.astype(jnp.float32)).astype(grads.dtype)

    right_sum = lax.ppermute(add(part(1, 0), from_left), "replica", rightward)
    left_sum = lax.ppermute(add(part(3, 1), from_right), "replica", leftward)
    return combine(
        jnp.reshape(me, (1,)).astype(jnp.int32),
        parts,
        right_plain,
        right_sum,
        left_plain,
        left_sum,
        ncols,
    )


def on_device(grads, block_owner, block_offsets, stat_left, stat_right, root_left, root_right):
    shards = lax.axis_size("shard")
    replicas = lax.axis_size("replica")
    devices = replicas * shards
    slots, width = stat_left.shape[:2]
    ncols = grads.shape[2] // width
    blocks = block_owner.shape[0]
    across = width // LANES
    groups = width // ROWS
    row = block_offsets[:, 0] // width
    col = block_offsets[:, 1] // width

    here = (col * shards + row)[None, :] == jnp.arange(blocks, dtype=jnp.int32)[:, None]
    owner_of = jnp.sum(jnp.where(here, block_owner[None, :], 0), axis=1)

    summed = reduce_rows(grads, replicas, ncols)
    summed, owner_of, source = lax.optimization_barrier((summed, owner_of, row * ncols + col))
    spread = lax.all_to_all(
        summed.reshape(shards, ncols, ROWS, LANES), "shard", split_axis=0, concat_axis=0, tiled=True
    )
    by_slot = to_slots(
        source, block_owner, spread.reshape(blocks, ROWS, LANES), devices * slots
    )
    everyone = ("replica", "shard")
    owned = lax.all_to_all(
        by_slot.reshape(devices, slots, ROWS, LANES),
        everyone,
        split_axis=0,
        concat_axis=0,
        tiled=True,
    ).reshape(groups, across, slots, ROWS, LANES)
    steer = steer_slots(owned, root_left, root_right)
    new_left, new_right = gram_slots(owned, stat_left, stat_right)
    returned = lax.all_to_all(
        steer.reshape(devices, slots, ROWS, LANES),
        everyone,
        split_axis=0,
        concat_axis=0,
        tiled=True,
    )
    by_place = pick(owner_of, returned.reshape(devices * slots, ROWS, LANES))
    home = lax.all_to_all(by_place, everyone, split_axis=0, concat_axis=0, tiled=True)
    direction = (
        home.reshape(groups, across, ROWS, LANES).transpose(0, 2, 1, 3).reshape(width, width)
    )
    return (new_left, new_right, direction)


def solution(mesh):
    placed = (
        P("replica", "shard", None),
        P(),
        P(),
        P(("replica", "shard"), None, None),
        P(("replica", "shard"), None, None),
        P(("replica", "shard"), None, None),
        P(("replica", "shard"), None, None),
    )
    return jax.shard_map(
        on_device,
        mesh=mesh,
        in_specs=placed,
        out_specs=(
            P(("replica", "shard"), None, None),
            P(("replica", "shard"), None, None),
            P("shard", "replica"),
        ),
        check_vma=False,
    )
```

time: 166 us -> 162 us (0.976)
  blocking collectives: 75.5 us -> 109 us
  waiting for transfers between devices: 47.1 us -> 26.9 us
  starting transfers between devices: 28 us -> 12.2 us
  local copies, waits for them, and re-layouts: 5.71 us -> 3.1 us
    all_to_all x0 -> x1, blocking collectives: none -> 32 us  [on_device(): lax.all_to_all(summed.reshape(shards, ncols, ROWS, LANES), 'shard', split...]
    all_to_all x1 -> x0, waiting for transfers between devices: 17.2 us -> none  [on_device(): lax.all_to_all(summed.reshape(shards, ncols, ROWS, LANES), 'shard', split...]
    all_to_all x1 -> x0, starting transfers between devices: 13.5 us -> none  [on_device(): lax.all_to_all(summed.reshape(shards, ncols, ROWS, LANES), 'shard', split...]
    unnamed x17 -> x13, local copies, waits for them, and re-layouts: 4.27 us -> 0.82 us
    ppermute x1, waiting for transfers between devices: 3.09 us -> 0.01 us  [reduce_rows(): right_sum = lax.ppermute(add(part(1, 0), from_left), 'replica', rightward)]
    ppermute x1, waiting for transfers between devices: 2.52 us -> 5.47 us  [reduce_rows(): left_sum = lax.ppermute(add(part(3, 1), from_right), 'replica', leftward)]
    ppermute x1, waiting for transfers between devices: 3.09 us -> 0.14 us  [reduce_rows(): right_plain = lax.ppermute(part(1, 1), 'replica', rightward)]
    ppermute x2, waiting for transfers between devices: 5.39 us -> 2.51 us  [the longest x1 1.48 us: reduce_rows(): from_right = lax.ppermute(far_left, 'replica', leftward)]
  transfers between devices with their start and end apart: 8 -> 7, of which waited for: 8 -> 6; matrix products, arithmetic and copies ran while one was open for 0% -> 1% of each run, Pallas kernels for 2% -> 3%
where the time goes in v2:
time: 162 us
  blocking collectives  109 us (67%)
  waiting for transfers between devices  26.9 us (17%)
  starting transfers between devices  12.2 us (8%)
  Pallas kernels  9.85 us (6%)
  local copies, waits for them, and re-layouts  3.1 us (2%)
    all_to_all x1, blocking collectives, on_device(): lax.all_to_all(by_slot.reshape(devices, slots, ROWS, LANES), everyone, sp...  40 us
    all_to_all x1, blocking collectives, on_device(): lax.all_to_all(steer.reshape(devices, slots, ROWS, LANES), everyone, spli...  36.9 us
    all_to_all x1, blocking collectives, on_device(): lax.all_to_all(summed.reshape(shards, ncols, ROWS, LANES), 'shard', split...  32 us
    all_to_all x1, waiting for transfers between devices, on_device(): lax.all_to_all(by_place, everyone, split_axis=0, concat_axis=0, tiled=True)  15.4 us
    ppermute x1, waiting for transfers between devices, reduce_rows(): left_sum = lax.ppermute(add(part(3, 1), from_right), 'replica', leftward)  5.47 us
    pallas_call x1, Pallas kernels, gram_slots(): pl.pallas_call(gram_kernel, out_shape=[jax.ShapeDtypeStruct(stat.shape, s...  5.37 us
    all_to_all x1, starting transfers between devices, on_device(): lax.all_to_all(by_place, everyone, split_axis=0, concat_axis=0, tiled=True)  5.19 us
    ppermute x1, waiting for transfers between devices, reduce_rows(): left_plain = lax.ppermute(part(3, 0), 'replica', leftward)  3.33 us
  transfers between devices with their start and end apart: 7, of which 6 were waited for; matrix products, arithmetic and copies ran while one was open for 1% of the time, Pallas kernels for 3%

profile of v2, /device:TPU:1, one launch (start us, length us, event | category | flops | bytes accessed | tf_op | source)
XLA Modules:
  0.0 162.0 jit_solution(15575542711220594796)
XLA Ops:
  0.6 0.0 copy-start.1
  0.6 0.0 copy-start.5
  0.7 0.0 copy-start.4
  0.7 1.2 dynamic-slice_bitcast_fusion.2
  1.9 2.1 %collective-permute-start.1 = (bf16[64,2048]{1,0:T(8,128)(2,1)S(1)}, bf16[64,2048]{1,0:T(8,128)(2,1)S(1)}, u32[]{:S(2)}, u32[]{:S(2)}) collective-permute-start(bf16[64,2048]{1,0:T(8,128)(2,1)S(1)} %get-tuple-element.12), channel_id=1, source_target_pairs={{0,64},{64,128},{128,192},{192,0},{1,65},{65,129},{129,193},{193,1... | collective-permute-start | bytes 786440 | tf_op jit(solution)/shard_map/ppermute | solution.py:213
  4.0 1.4 collective-permute-start.4
  5.4 1.1 dynamic-slice_bitcast_fusion
  6.4 1.5 collective-permute-start.3
  7.9 0.1 collective-permute-start
  8.0 0.0 copy-done.5
  8.0 1.0 collective-permute-done.1
  9.0 1.5 collective-permute-done.4
  10.5 0.0 copy-done.1
  10.5 0.1 fusion
  10.6 2.0 %collective-permute-start.5 = (bf16[64,2048]{1,0:T(8,128)(2,1)S(1)}, bf16[64,2048]{1,0:T(8,128)(2,1)S(1)}, u32[]{:S(2)}, u32[]{:S(2)}) collective-permute-start(bf16[64,2048]{1,0:T(8,128)(2,1)S(1)} %get-tuple-element.22), channel_id=1, source_target_pairs={{0,192},{64,0},{128,64},{192,128},{1,193},{65,1},{129,65},{193,129... | collective-permute-start | bytes 786440 | tf_op jit(solution)/shard_map/ppermute | solution.py:222
  12.7 0.0 collective-permute-start.2
  12.7 0.0 copy-done.4
  12.7 0.1 select_reduce_fusion.index_ref
  12.8 3.3 %collective-permute-done.3.refs_2_ = bf16[64,2048]{1,0:T(8,128)(2,1)S(1)} collective-permute-done((bf16[64,2048]{1,0:T(8,128)(2,1)S(1)}, bf16[64,2048]{1,0:T(8,128)(2,1)S(1)}, u32[]{:S(2)}, u32[]{:S(2)}) %collective-permute-start.3) | collective-permute-done | bytes 262176 | tf_op jit(solution)/shard_map/ppermute | solution.py:216
  16.1 0.1 collective-permute-done.refs_0_
  16.3 5.5 %collective-permute-done.5.refs_3_ = bf16[64,2048]{1,0:T(8,128)(2,1)S(1)} collective-permute-done((bf16[64,2048]{1,0:T(8,128)(2,1)S(1)}, bf16[64,2048]{1,0:T(8,128)(2,1)S(1)}, u32[]{:S(2)}, u32[]{:S(2)}) %collective-permute-start.5) | collective-permute-done | bytes 262176 | tf_op jit(solution)/shard_map/ppermute | solution.py:222
  21.7 0.0 collective-permute-done.2.refs_1_
  21.7 0.2 combine.1
  22.0 32.0 %all_to_all.20 = bf16[64,4,8,128]{3,2,1,0:T(8,128)(2,1)S(1)} all-to-all(bf16[64,4,8,128]{3,2,1,0:T(8,128)(2,1)S(1)} %bitcast.39), channel_id=1, replica_groups=mesh['replica'=4,'shard'=64] {'shard'}, dimensions={0} | all-to-all | bytes 1048576 | tf_op jit(solution)/shard_map/all_to_all | solution.py:251
  53.9 0.0 copy-start.2
  53.9 0.0 copy-start.3
  53.9 1.3 to_slots.1
  55.2 40.0 %all_to_all.21 = bf16[256,2,8,128]{3,2,1,0:T(8,128)(2,1)S(1)} all-to-all(bf16[256,2,8,128]{3,2,1,0:T(8,128)(2,1)S(1)} %bitcast.35), channel_id=1, replica_groups=mesh['replica'=4,'shard'=64] {'replica','shard'}, dimensions={0} | all-to-all | bytes 2097152 | tf_op jit(solution)/shard_map/all_to_all | solution.py:258
  95.3 0.0 copy-start
  95.3 0.0 copy-done.2
  95.3 0.0 copy-done.3
  95.3 1.4 steer.1
  96.7 0.0 copy-done
  96.7 36.9 %all_to_all.22 = bf16[256,2,8,128]{3,2,1,0:T(8,128)(2,1)S(1)} all-to-all(bf16[256,2,8,128]{3,2,1,0:T(8,128)(2,1)S(1)} %bitcast.37), channel_id=1, replica_groups=mesh['replica'=4,'shard'=64] {'replica','shard'}, dimensions={0} | all-to-all | bytes 2097152 | tf_op jit(solution)/shard_map/all_to_all | solution.py:267
  133.6 1.6 pick.1
  135.2 5.2 %all-to-all-start.3 = ((bf16[256,8,128]{2,1,0:T(8,128)(2,1)}), bf16[256,8,128]{2,1,0:T(8,128)(2,1)S(1)}, u32[]{:S(2)}, u32[]{:S(2)}) async-start(bf16[256,8,128]{2,1,0:T(8,128)(2,1)} %pick.1), calls=%async_computation.3 | async-start | bytes 1048576 | tf_op jit(solution)/shard_map/all_to_all | solution.py:275
  140.4 5.4 %gram.1 = (f32[2,512,512]{2,1,0:T(8,128)}, f32[2,512,512]{2,1,0:T(8,128)}) custom-call(bf16[64,4,2,8,128]{4,3,2,1,0:T(8,128)(2,1)} %bitcast.30, f32[2,512,512]{2,1,0:T(8,128)} %left_ref.2, f32[2,512,512]{2,1,0:T(8,128)} %right_ref.2), custom_call_target="tpu_custom_call" | custom-call | flops 1073741824 | bytes 9437184 | tf_op jit(solution)/shard_map/gram/pallas_call | solution.py:183
  145.7 15.4 %all-to-all-done.3 = bf16[256,8,128]{2,1,0:T(8,128)(2,1)S(1)} async-done(((bf16[256,8,128]{2,1,0:T(8,128)(2,1)}), bf16[256,8,128]{2,1,0:T(8,128)(2,1)S(1)}, u32[]{:S(2)}, u32[]{:S(2)}) %all-to-all-start.3) | async-done | bytes 524320 | tf_op jit(solution)/shard_map/all_to_all | solution.py:275
  161.2 0.8 copy.11
  (3 shorter events, 0.0 us)
Async XLA Ops:
  0.6 9.9 %copy-start.1 = (bf16[1,512,2048]{2,1,0:T(8,128)(2,1)S(1)}, bf16[1,512,2048]{2,1,0:T(8,128)(2,1)}, u32[]{:S(2)}) copy-start(bf16[1,512,2048]{2,1,0:T(8,128)(2,1)} %param.7) | copy-start | bytes 6291460
  0.6 7.3 %copy-start.5 = (s32[256,2]{0,1:T(2,128)S(1)}, s32[256,2]{0,1:T(2,128)}, u32[]{:S(2)}) copy-start(s32[256,2]{0,1:T(2,128)} %param.9) | copy-start | bytes 6148
  0.7 12.0 %copy-start.4 = (s32[256]{0:T(256)S(1)}, s32[256]{0:T(256)}, u32[]{:S(2)}) copy-start(s32[256]{0:T(256)} %target_ref.1) | copy-start | bytes 3076
  1.9 7.1 %collective-permute-start.1 = (bf16[64,2048]{1,0:T(8,128)(2,1)S(1)}, bf16[64,2048]{1,0:T(8,128)(2,1)S(1)}, u32[]{:S(2)}, u32[]{:S(2)}) collective-permute-start(bf16[64,2048]{1,0:T(8,128)(2,1)S(1)} %get-tuple-element.12), channel_id=1, source_target_pairs={{0,64},{64,128},{128,192},{192,0},{1,65},{65,129},{129,193},{193,1... | collective-permute-start | bytes 786440 | tf_op jit(solution)/shard_map/ppermute | solution.py:213
  4.0 6.5 %collective-permute-start.4 = (bf16[64,2048]{1,0:T(8,128)(2,1)S(1)}, bf16[64,2048]{1,0:T(8,128)(2,1)S(1)}, u32[]{:S(2)}, u32[]{:S(2)}) collective-permute-start(bf16[64,2048]{1,0:T(8,128)(2,1)S(1)} %get-tuple-element.13), channel_id=1, source_target_pairs={{0,192},{64,0},{128,64},{192,128},{1,193},{65,1},{129,65},{193,129... | collective-permute-start | bytes 786440 | tf_op jit(solution)/shard_map/ppermute | solution.py:214
  6.4 9.7 %collective-permute-start.3 = (bf16[64,2048]{1,0:T(8,128)(2,1)S(1)}, bf16[64,2048]{1,0:T(8,128)(2,1)S(1)}, u32[]{:S(2)}, u32[]{:S(2)}) collective-permute-start(bf16[64,2048]{1,0:T(8,128)(2,1)S(1)} %get-tuple-element.24), channel_id=1, source_target_pairs={{0,192},{64,0},{128,64},{192,128},{1,193},{65,1},{129,65},{193,129... | collective-permute-start | bytes 786440 | tf_op jit(solution)/shard_map/ppermute | solution.py:216
  7.9 8.4 %collective-permute-start = (bf16[64,2048]{1,0:T(8,128)(2,1)S(1)}, bf16[64,2048]{1,0:T(8,128)(2,1)S(1)}, u32[]{:S(2)}, u32[]{:S(2)}) collective-permute-start(bf16[64,2048]{1,0:T(8,128)(2,1)S(1)} %get-tuple-element.25), channel_id=1, source_target_pairs={{0,64},{64,128},{128,192},{192,0},{1,65},{65,129},{129,193},{193,1... | collective-permute-start | bytes 786440 | tf_op jit(solution)/shard_map/ppermute | solution.py:215
  10.6 11.1 %collective-permute-start.5 = (bf16[64,2048]{1,0:T(8,128)(2,1)S(1)}, bf16[64,2048]{1,0:T(8,128)(2,1)S(1)}, u32[]{:S(2)}, u32[]{:S(2)}) collective-permute-start(bf16[64,2048]{1,0:T(8,128)(2,1)S(1)} %get-tuple-element.22), channel_id=1, source_target_pairs={{0,192},{64,0},{128,64},{192,128},{1,193},{65,1},{129,65},{193,129... | collective-permute-start | bytes 786440 | tf_op jit(solution)/shard_map/ppermute | solution.py:222
  12.7 9.1 %collective-permute-start.2 = (bf16[64,2048]{1,0:T(8,128)(2,1)S(1)}, bf16[64,2048]{1,0:T(8,128)(2,1)S(1)}, u32[]{:S(2)}, u32[]{:S(2)}) collective-permute-start(bf16[64,2048]{1,0:T(8,128)(2,1)S(1)} %get-tuple-element.23), channel_id=1, source_target_pairs={{0,64},{64,128},{128,192},{192,0},{1,65},{65,129},{129,193},{193,1... | collective-permute-start | bytes 786440 | tf_op jit(solution)/shard_map/ppermute | solution.py:221
  53.9 41.3 %copy-start.2 = (bf16[2,512,512]{2,1,0:T(8,128)(2,1)S(1)}, bf16[2,512,512]{2,1,0:T(8,128)(2,1)}, u32[]{:S(2)}) copy-start(bf16[2,512,512]{2,1,0:T(8,128)(2,1)} %left_ref.3) | copy-start | bytes 3145732
  53.9 41.3 %copy-start.3 = (bf16[2,512,512]{2,1,0:T(8,128)(2,1)S(1)}, bf16[2,512,512]{2,1,0:T(8,128)(2,1)}, u32[]{:S(2)}) copy-start(bf16[2,512,512]{2,1,0:T(8,128)(2,1)} %right_ref.3) | copy-start | bytes 3145732
  95.3 1.4 copy-start
  135.2 26.0 %all-to-all-start.3 = ((bf16[256,8,128]{2,1,0:T(8,128)(2,1)}), bf16[256,8,128]{2,1,0:T(8,128)(2,1)S(1)}, u32[]{:S(2)}, u32[]{:S(2)}) async-start(bf16[256,8,128]{2,1,0:T(8,128)(2,1)} %pick.1), calls=%async_computation.3 | async-start | bytes 1048576 | tf_op jit(solution)/shard_map/all_to_all | solution.py:275

commit v3 on v2

--- a/solution.py
+++ b/solution.py
@@ -11,6 +11,9 @@
 LANES = 128
 UNROLL = 16
 PARTS = 4
+FAR_SHARD = 40
+FAR_DEVICE = 168
+STRIDE = 2
 VMEM_LIMIT = 16 * 1024 * 1024
 GRAM_VMEM = 62 * 1024 * 1024
 IN_VMEM = pl.BlockSpec(memory_space=pltpu.VMEM)
@@ -34,8 +37,9 @@
                     + first[:, lanes].astype(jnp.float32)
                     + second[:, lanes].astype(jnp.float32)
                 ).astype(out_ref.dtype)
-                rows = pl.ds(side * groups, groups)
-                out_ref[rows, tile, block] = total.reshape(groups, ROWS, LANES)
+                for group in range(groups):
+                    row = (side * groups + group) ^ (FAR_SHARD // across)
+                    out_ref[row, tile, block] = total[group * ROWS : (group + 1) * ROWS]
 
 
 def combine(me, parts, right_plain, right_sum, left_plain, left_sum, ncols):
@@ -129,8 +133,10 @@
         steer = jnp.dot(left_ref[slot], right_side, preferred_element_type=jnp.float32)
         steer = steer.astype(out_ref.dtype)
         for tile in range(across):
-            piece = steer[:, tile * LANES : (tile + 1) * LANES]
-            out_ref[:, tile, slot] = piece.reshape(groups, ROWS, LANES)
+            piece = steer[:, tile * LANES : (tile + 1) * LANES].reshape(groups, ROWS, LANES)
+            for group in range(0, groups, STRIDE):
+                rows = pl.ds(group ^ (FAR_DEVICE // across), STRIDE)
+                out_ref[rows, tile, slot] = piece[group : group + STRIDE]
 
 
 def gram_kernel(tiles_ref, left_ref, right_ref, new_left_ref, new_right_ref, held, in_sems, out_sems):
@@ -243,13 +249,21 @@
     row = block_offsets[:, 0] // width
     col = block_offsets[:, 1] // width
 
-    here = (col * shards + row)[None, :] == jnp.arange(blocks, dtype=jnp.int32)[:, None]
+    target = (col * shards + row) ^ FAR_DEVICE
+    here = target[None, :] == jnp.arange(blocks, dtype=jnp.int32)[:, None]
     owner_of = jnp.sum(jnp.where(here, block_owner[None, :], 0), axis=1)
 
     summed = reduce_rows(grads, replicas, ncols)
-    summed, owner_of, source = lax.optimization_barrier((summed, owner_of, row * ncols + col))
+    summed, owner_of, source = lax.optimization_barrier(
+        (summed, owner_of, (row ^ FAR_SHARD) * ncols + col)
+    )
     spread = lax.all_to_all(
-        summed.reshape(shards, ncols, ROWS, LANES), "shard", split_axis=0, concat_axis=0, tiled=True
+        summed.reshape(shards, ncols, ROWS, LANES),
+        "shard",
+        split_axis=0,
+        concat_axis=0,
+        axis_index_groups=[[index ^ FAR_SHARD for index in range(shards)]],
+        tiled=True,
     )
     by_slot = to_slots(
         source, block_owner, spread.reshape(blocks, ROWS, LANES), devices * slots
@@ -272,7 +286,14 @@
         tiled=True,
     )
     by_place = pick(owner_of, returned.reshape(devices * slots, ROWS, LANES))
-    home = lax.all_to_all(by_place, everyone, split_axis=0, concat_axis=0, tiled=True)
+    home = lax.all_to_all(
+        by_place,
+        everyone,
+        split_axis=0,
+        concat_axis=0,
+        axis_index_groups=[[index ^ FAR_DEVICE for index in range(devices)]],
+        tiled=True,
+    )
     direction = (
         home.reshape(groups, across, ROWS, LANES).transpose(0, 2, 1, 3).reshape(width, width)
     )

time: 162 us -> 160 us (0.988)
    all_to_all x1, blocking collectives: 32 us -> 29.4 us  [on_device(): lax.all_to_all(summed.reshape(shards, ncols, ROWS, LANES), 'shard', split...]
    all_to_all x1, blocking collectives: 40 us -> 41.8 us  [on_device(): lax.all_to_all(by_slot.reshape(devices, slots, ROWS, LANES), everyone, sp...]
where the time goes in v3:
time: 160 us
  blocking collectives  108 us (68%)
  waiting for transfers between devices  25.9 us (16%)
  starting transfers between devices  12.2 us (8%)
  Pallas kernels  9.85 us (6%)
  local copies, waits for them, and re-layouts  3.1 us (2%)
    all_to_all x1, blocking collectives, on_device(): lax.all_to_all(by_slot.reshape(devices, slots, ROWS, LANES), everyone, sp...  41.8 us
    all_to_all x1, blocking collectives, on_device(): lax.all_to_all(steer.reshape(devices, slots, ROWS, LANES), everyone, spli...  36.9 us
    all_to_all x1, blocking collectives, on_device(): lax.all_to_all(summed.reshape(shards, ncols, ROWS, LANES), 'shard', split...  29.4 us
    all_to_all x1, waiting for transfers between devices, on_device(): lax.all_to_all(by_place, everyone, split_axis=0, concat_axis=0, axis_inde...  14.4 us
    ppermute x1, waiting for transfers between devices, reduce_rows(): left_sum = lax.ppermute(add(part(3, 1), from_right), 'replica', leftward)  5.47 us
    pallas_call x1, Pallas kernels, gram_slots(): pl.pallas_call(gram_kernel, out_shape=[jax.ShapeDtypeStruct(stat.shape, s...  5.37 us
    all_to_all x1, starting transfers between devices, on_device(): lax.all_to_all(by_place, everyone, split_axis=0, concat_axis=0, axis_inde...  5.19 us
    ppermute x1, waiting for transfers between devices, reduce_rows(): left_plain = lax.ppermute(part(3, 0), 'replica', leftward)  3.33 us
  transfers between devices with their start and end apart: 7, of which 6 were waited for; matrix products, arithmetic and copies ran while one was open for 1% of the time, Pallas kernels for 3%

profile of v3, /device:TPU:1, one launch (start us, length us, event | category | flops | bytes accessed | tf_op | source)
XLA Modules:
  0.0 160.2 jit_solution(7578347611088777241)
XLA Ops:
  0.6 0.0 copy-start.1
  0.6 0.0 copy-start.5
  0.7 0.0 copy-start.4
  0.7 1.2 dynamic-slice_bitcast_fusion.2
  1.9 2.1 %collective-permute-start.1 = (bf16[64,2048]{1,0:T(8,128)(2,1)S(1)}, bf16[64,2048]{1,0:T(8,128)(2,1)S(1)}, u32[]{:S(2)}, u32[]{:S(2)}) collective-permute-start(bf16[64,2048]{1,0:T(8,128)(2,1)S(1)} %get-tuple-element.12), channel_id=1, source_target_pairs={{0,64},{64,128},{128,192},{192,0},{1,65},{65,129},{129,193},{193,1... | collective-permute-start | bytes 786440 | tf_op jit(solution)/shard_map/ppermute | solution.py:219
  4.0 1.4 collective-permute-start.4
  5.4 1.1 dynamic-slice_bitcast_fusion
  6.4 1.5 collective-permute-start.3
  7.9 0.1 collective-permute-start
  8.0 0.0 copy-done.5
  8.0 1.0 collective-permute-done.1
  9.0 1.5 collective-permute-done.4
  10.5 0.0 copy-done.1
  10.5 0.1 fusion
  10.6 2.0 %collective-permute-start.5 = (bf16[64,2048]{1,0:T(8,128)(2,1)S(1)}, bf16[64,2048]{1,0:T(8,128)(2,1)S(1)}, u32[]{:S(2)}, u32[]{:S(2)}) collective-permute-start(bf16[64,2048]{1,0:T(8,128)(2,1)S(1)} %get-tuple-element.22), channel_id=1, source_target_pairs={{0,192},{64,0},{128,64},{192,128},{1,193},{65,1},{129,65},{193,129... | collective-permute-start | bytes 786440 | tf_op jit(solution)/shard_map/ppermute | solution.py:228
  12.7 0.0 collective-permute-start.2
  12.7 0.0 copy-done.4
  12.7 0.1 select_reduce_fusion.index_ref
  12.8 3.3 %collective-permute-done.3.refs_2_ = bf16[64,2048]{1,0:T(8,128)(2,1)S(1)} collective-permute-done((bf16[64,2048]{1,0:T(8,128)(2,1)S(1)}, bf16[64,2048]{1,0:T(8,128)(2,1)S(1)}, u32[]{:S(2)}, u32[]{:S(2)}) %collective-permute-start.3) | collective-permute-done | bytes 262176 | tf_op jit(solution)/shard_map/ppermute | solution.py:222
  16.1 0.1 collective-permute-done.refs_0_
  16.3 5.5 %collective-permute-done.5.refs_3_ = bf16[64,2048]{1,0:T(8,128)(2,1)S(1)} collective-permute-done((bf16[64,2048]{1,0:T(8,128)(2,1)S(1)}, bf16[64,2048]{1,0:T(8,128)(2,1)S(1)}, u32[]{:S(2)}, u32[]{:S(2)}) %collective-permute-start.5) | collective-permute-done | bytes 262176 | tf_op jit(solution)/shard_map/ppermute | solution.py:228
  21.7 0.0 collective-permute-done.2.refs_1_
  21.7 0.2 combine.1
  22.0 29.4 %all_to_all.20 = bf16[64,4,8,128]{3,2,1,0:T(8,128)(2,1)S(1)} all-to-all(bf16[64,4,8,128]{3,2,1,0:T(8,128)(2,1)S(1)} %bitcast.39), channel_id=1, replica_groups={{40,41,42,43,44,45,46,47,32,33,34,35,36,37,38,39,56,57,58,59,60,61,62,6..., dimensions={0} | all-to-all | bytes 1048576 | tf_op jit(solution)/shard_map/all_to_all | solution.py:260
  51.3 0.0 copy-start.2
  51.3 0.0 copy-start.3
  51.3 1.3 to_slots.1
  52.6 41.8 %all_to_all.21 = bf16[256,2,8,128]{3,2,1,0:T(8,128)(2,1)S(1)} all-to-all(bf16[256,2,8,128]{3,2,1,0:T(8,128)(2,1)S(1)} %bitcast.35), channel_id=1, replica_groups=mesh['replica'=4,'shard'=64] {'replica','shard'}, dimensions={0} | all-to-all | bytes 2097152 | tf_op jit(solution)/shard_map/all_to_all | solution.py:272
  94.4 0.0 copy-start
  94.5 0.0 copy-done.2
  94.5 0.0 copy-done.3
  94.5 1.4 steer.1
  95.9 0.0 copy-done
  95.9 36.9 %all_to_all.22 = bf16[256,2,8,128]{3,2,1,0:T(8,128)(2,1)S(1)} all-to-all(bf16[256,2,8,128]{3,2,1,0:T(8,128)(2,1)S(1)} %bitcast.37), channel_id=1, replica_groups=mesh['replica'=4,'shard'=64] {'replica','shard'}, dimensions={0} | all-to-all | bytes 2097152 | tf_op jit(solution)/shard_map/all_to_all | solution.py:281
  132.8 1.6 pick.1
  134.4 5.2 %all-to-all-start.3 = ((bf16[256,8,128]{2,1,0:T(8,128)(2,1)}), bf16[256,8,128]{2,1,0:T(8,128)(2,1)S(1)}, u32[]{:S(2)}, u32[]{:S(2)}) async-start(bf16[256,8,128]{2,1,0:T(8,128)(2,1)} %pick.1), calls=%async_computation.3 | async-start | bytes 1048576 | tf_op jit(solution)/shard_map/all_to_all | solution.py:289
  139.6 5.4 %gram.1 = (f32[2,512,512]{2,1,0:T(8,128)}, f32[2,512,512]{2,1,0:T(8,128)}) custom-call(bf16[64,4,2,8,128]{4,3,2,1,0:T(8,128)(2,1)} %bitcast.30, f32[2,512,512]{2,1,0:T(8,128)} %left_ref.2, f32[2,512,512]{2,1,0:T(8,128)} %right_ref.2), custom_call_target="tpu_custom_call" | custom-call | flops 1073741824 | bytes 9437184 | tf_op jit(solution)/shard_map/gram/pallas_call | solution.py:189
  144.9 14.4 %all-to-all-done.3 = bf16[256,8,128]{2,1,0:T(8,128)(2,1)S(1)} async-done(((bf16[256,8,128]{2,1,0:T(8,128)(2,1)}), bf16[256,8,128]{2,1,0:T(8,128)(2,1)S(1)}, u32[]{:S(2)}, u32[]{:S(2)}) %all-to-all-start.3) | async-done | bytes 524320 | tf_op jit(solution)/shard_map/all_to_all | solution.py:289
  159.4 0.8 copy.11
  (3 shorter events, 0.0 us)
Async XLA Ops:
  0.6 9.9 %copy-start.1 = (bf16[1,512,2048]{2,1,0:T(8,128)(2,1)S(1)}, bf16[1,512,2048]{2,1,0:T(8,128)(2,1)}, u32[]{:S(2)}) copy-start(bf16[1,512,2048]{2,1,0:T(8,128)(2,1)} %param.7) | copy-start | bytes 6291460
  0.6 7.3 %copy-start.5 = (s32[256,2]{0,1:T(2,128)S(1)}, s32[256,2]{0,1:T(2,128)}, u32[]{:S(2)}) copy-start(s32[256,2]{0,1:T(2,128)} %param.9) | copy-start | bytes 6148
  0.7 12.0 %copy-start.4 = (s32[256]{0:T(256)S(1)}, s32[256]{0:T(256)}, u32[]{:S(2)}) copy-start(s32[256]{0:T(256)} %target_ref.1) | copy-start | bytes 3076
  1.9 7.1 %collective-permute-start.1 = (bf16[64,2048]{1,0:T(8,128)(2,1)S(1)}, bf16[64,2048]{1,0:T(8,128)(2,1)S(1)}, u32[]{:S(2)}, u32[]{:S(2)}) collective-permute-start(bf16[64,2048]{1,0:T(8,128)(2,1)S(1)} %get-tuple-element.12), channel_id=1, source_target_pairs={{0,64},{64,128},{128,192},{192,0},{1,65},{65,129},{129,193},{193,1... | collective-permute-start | bytes 786440 | tf_op jit(solution)/shard_map/ppermute | solution.py:219
  4.0 6.5 %collective-permute-start.4 = (bf16[64,2048]{1,0:T(8,128)(2,1)S(1)}, bf16[64,2048]{1,0:T(8,128)(2,1)S(1)}, u32[]{:S(2)}, u32[]{:S(2)}) collective-permute-start(bf16[64,2048]{1,0:T(8,128)(2,1)S(1)} %get-tuple-element.13), channel_id=1, source_target_pairs={{0,192},{64,0},{128,64},{192,128},{1,193},{65,1},{129,65},{193,129... | collective-permute-start | bytes 786440 | tf_op jit(solution)/shard_map/ppermute | solution.py:220
  6.4 9.7 %collective-permute-start.3 = (bf16[64,2048]{1,0:T(8,128)(2,1)S(1)}, bf16[64,2048]{1,0:T(8,128)(2,1)S(1)}, u32[]{:S(2)}, u32[]{:S(2)}) collective-permute-start(bf16[64,2048]{1,0:T(8,128)(2,1)S(1)} %get-tuple-element.24), channel_id=1, source_target_pairs={{0,192},{64,0},{128,64},{192,128},{1,193},{65,1},{129,65},{193,129... | collective-permute-start | bytes 786440 | tf_op jit(solution)/shard_map/ppermute | solution.py:222
  7.9 8.4 %collective-permute-start = (bf16[64,2048]{1,0:T(8,128)(2,1)S(1)}, bf16[64,2048]{1,0:T(8,128)(2,1)S(1)}, u32[]{:S(2)}, u32[]{:S(2)}) collective-permute-start(bf16[64,2048]{1,0:T(8,128)(2,1)S(1)} %get-tuple-element.25), channel_id=1, source_target_pairs={{0,64},{64,128},{128,192},{192,0},{1,65},{65,129},{129,193},{193,1... | collective-permute-start | bytes 786440 | tf_op jit(solution)/shard_map/ppermute | solution.py:221
  10.6 11.1 %collective-permute-start.5 = (bf16[64,2048]{1,0:T(8,128)(2,1)S(1)}, bf16[64,2048]{1,0:T(8,128)(2,1)S(1)}, u32[]{:S(2)}, u32[]{:S(2)}) collective-permute-start(bf16[64,2048]{1,0:T(8,128)(2,1)S(1)} %get-tuple-element.22), channel_id=1, source_target_pairs={{0,192},{64,0},{128,64},{192,128},{1,193},{65,1},{129,65},{193,129... | collective-permute-start | bytes 786440 | tf_op jit(solution)/shard_map/ppermute | solution.py:228
  12.7 9.1 %collective-permute-start.2 = (bf16[64,2048]{1,0:T(8,128)(2,1)S(1)}, bf16[64,2048]{1,0:T(8,128)(2,1)S(1)}, u32[]{:S(2)}, u32[]{:S(2)}) collective-permute-start(bf16[64,2048]{1,0:T(8,128)(2,1)S(1)} %get-tuple-element.23), channel_id=1, source_target_pairs={{0,64},{64,128},{128,192},{192,0},{1,65},{65,129},{129,193},{193,1... | collective-permute-start | bytes 786440 | tf_op jit(solution)/shard_map/ppermute | solution.py:227
  51.3 43.1 %copy-start.2 = (bf16[2,512,512]{2,1,0:T(8,128)(2,1)S(1)}, bf16[2,512,512]{2,1,0:T(8,128)(2,1)}, u32[]{:S(2)}) copy-start(bf16[2,512,512]{2,1,0:T(8,128)(2,1)} %left_ref.3) | copy-start | bytes 3145732
  51.3 43.1 %copy-start.3 = (bf16[2,512,512]{2,1,0:T(8,128)(2,1)S(1)}, bf16[2,512,512]{2,1,0:T(8,128)(2,1)}, u32[]{:S(2)}) copy-start(bf16[2,512,512]{2,1,0:T(8,128)(2,1)} %right_ref.3) | copy-start | bytes 3145732
  94.4 1.4 copy-start
  134.4 25.0 %all-to-all-start.3 = ((bf16[256,8,128]{2,1,0:T(8,128)(2,1)}), bf16[256,8,128]{2,1,0:T(8,128)(2,1)S(1)}, u32[]{:S(2)}, u32[]{:S(2)}) async-start(bf16[256,8,128]{2,1,0:T(8,128)(2,1)} %pick.1), calls=%async_computation.3 | async-start | bytes 1048576 | tf_op jit(solution)/shard_map/all_to_all | solution.py:289

commit v4 on v3

--- a/solution.py
+++ b/solution.py
@@ -9,7 +9,7 @@
 
 ROWS = 8
 LANES = 128
-UNROLL = 16
+UNROLL = 32
 PARTS = 4
 FAR_SHARD = 40
 FAR_DEVICE = 168
@@ -55,31 +55,28 @@
     )(me, parts, right_plain, right_sum, left_plain, left_sum)
 
 
-def place_rows(source_ref, target_ref, in_ref, out_ref, begin, count):
+def to_slots_kernel(target_ref, in_ref, out_ref):
+    out_ref[...] = jnp.zeros_like(out_ref)
+
     def step(group, carry):
-        rows = [begin + group * UNROLL + offset for offset in range(UNROLL)]
-        pieces = [in_ref[source_ref[row]] for row in rows]
+        rows = [group * UNROLL + offset for offset in range(UNROLL)]
+        pieces = [in_ref[row] for row in rows]
         for row, piece in zip(rows, pieces):
             out_ref[target_ref[row]] = piece
         return carry
 
-    lax.fori_loop(0, count // UNROLL, step, 0)
-
-
-def to_slots_kernel(source_ref, target_ref, in_ref, out_ref):
-    out_ref[...] = jnp.zeros_like(out_ref)
-    place_rows(source_ref, target_ref, in_ref, out_ref, 0, source_ref.shape[0])
-
-
-def to_slots(source, target, tiles, count):
+    lax.fori_loop(0, target_ref.shape[0] // UNROLL, step, 0)
+
+
+def to_slots(target, tiles, count):
     return pl.pallas_call(
         to_slots_kernel,
         out_shape=jax.ShapeDtypeStruct((count,) + tiles.shape[1:], tiles.dtype),
-        in_specs=[IN_SMEM, IN_SMEM, IN_VMEM],
+        in_specs=[IN_SMEM, IN_VMEM],
         out_specs=IN_VMEM,
         compiler_params=PARAMS,
         name="to_slots",
-    )(source, target, tiles)
+    )(target, tiles)
 
 
 def pick_kernel(index_ref, in_ref, out_ref, filled, sems):
@@ -249,14 +246,16 @@
     row = block_offsets[:, 0] // width
     col = block_offsets[:, 1] // width
 
-    target = (col * shards + row) ^ FAR_DEVICE
-    here = target[None, :] == jnp.arange(blocks, dtype=jnp.int32)[:, None]
-    owner_of = jnp.sum(jnp.where(here, block_owner[None, :], 0), axis=1)
+
+    def owners_by(place):
+        here = place[None, :] == jnp.arange(blocks, dtype=jnp.int32)[:, None]
+        return jnp.sum(jnp.where(here, block_owner[None, :], 0), axis=1)
+
+    by_source = owners_by((row ^ FAR_SHARD) * ncols + col)
+    by_home = owners_by((col * shards + row) ^ FAR_DEVICE)
 
     summed = reduce_rows(grads, replicas, ncols)
-    summed, owner_of, source = lax.optimization_barrier(
-        (summed, owner_of, (row ^ FAR_SHARD) * ncols + col)
-    )
+    summed, by_source, by_home = lax.optimization_barrier((summed, by_source, by_home))
     spread = lax.all_to_all(
         summed.reshape(shards, ncols, ROWS, LANES),
         "shard",
@@ -265,9 +264,7 @@
         axis_index_groups=[[index ^ FAR_SHARD for index in range(shards)]],
         tiled=True,
     )
-    by_slot = to_slots(
-        source, block_owner, spread.reshape(blocks, ROWS, LANES), devices * slots
-    )
+    by_slot = to_slots(by_source, spread.reshape(blocks, ROWS, LANES), devices * slots)
     everyone = ("replica", "shard")
     owned = lax.all_to_all(
         by_slot.reshape(devices, slots, ROWS, LANES),
@@ -285,7 +282,7 @@
         concat_axis=0,
         tiled=True,
     )
-    by_place = pick(owner_of, returned.reshape(devices * slots, ROWS, LANES))
+    by_place = pick(by_home, returned.reshape(devices * slots, ROWS, LANES))
     home = lax.all_to_all(
         by_place,
         everyone,

time: 160 us -> 160 us (level)
  no operation moved by 1% of the time
where the time goes in v4:
time: 160 us
  blocking collectives  108 us (68%)
  waiting for transfers between devices  25.9 us (16%)
  starting transfers between devices  12.2 us (8%)
  Pallas kernels  9.51 us (6%)
  local copies, waits for them, and re-layouts  3.1 us (2%)
    all_to_all x1, blocking collectives, on_device(): lax.all_to_all(by_slot.reshape(devices, slots, ROWS, LANES), everyone, sp...  41.8 us
    all_to_all x1, blocking collectives, on_device(): lax.all_to_all(steer.reshape(devices, slots, ROWS, LANES), everyone, spli...  36.9 us
    all_to_all x1, blocking collectives, on_device(): lax.all_to_all(summed.reshape(shards, ncols, ROWS, LANES), 'shard', split...  29.4 us
    all_to_all x1, waiting for transfers between devices, on_device(): lax.all_to_all(by_place, everyone, split_axis=0, concat_axis=0, axis_inde...  14.4 us
    ppermute x1, waiting for transfers between devices, reduce_rows(): left_sum = lax.ppermute(add(part(3, 1), from_right), 'replica', leftward)  5.47 us
    pallas_call x1, Pallas kernels, gram_slots(): pl.pallas_call(gram_kernel, out_shape=[jax.ShapeDtypeStruct(stat.shape, s...  5.37 us
    all_to_all x1, starting transfers between devices, on_device(): lax.all_to_all(by_place, everyone, split_axis=0, concat_axis=0, axis_inde...  5.19 us
    ppermute x1, waiting for transfers between devices, reduce_rows(): left_plain = lax.ppermute(part(3, 0), 'replica', leftward)  3.3 us
  transfers between devices with their start and end apart: 7, of which 6 were waited for; matrix products, arithmetic and copies ran while one was open for 1% of the time, Pallas kernels for 3%

profile of v4, /device:TPU:1, one launch (start us, length us, event | category | flops | bytes accessed | tf_op | source)
XLA Modules:
  0.0 159.8 jit_solution(5974418007600110367)
XLA Ops:
  0.6 0.0 copy-start.1
  0.6 0.0 copy-start.4
  0.7 0.0 copy-start.5
  0.7 1.2 dynamic-slice_bitcast_fusion.2
  1.9 2.1 %collective-permute-start.1 = (bf16[64,2048]{1,0:T(8,128)(2,1)S(1)}, bf16[64,2048]{1,0:T(8,128)(2,1)S(1)}, u32[]{:S(2)}, u32[]{:S(2)}) collective-permute-start(bf16[64,2048]{1,0:T(8,128)(2,1)S(1)} %get-tuple-element.12), channel_id=1, source_target_pairs={{0,64},{64,128},{128,192},{192,0},{1,65},{65,129},{129,193},{193,1... | collective-permute-start | bytes 786440 | tf_op jit(solution)/shard_map/ppermute | solution.py:216
  4.0 1.4 collective-permute-start.4
  5.4 1.1 dynamic-slice_bitcast_fusion
  6.4 1.5 collective-permute-start.3
  7.9 0.1 collective-permute-start
  8.0 0.0 copy-done.4
  8.0 1.0 collective-permute-done.1
  9.0 1.5 collective-permute-done.4
  10.5 0.0 copy-done.1
  10.5 0.1 fusion
  10.6 2.0 %collective-permute-start.5 = (bf16[64,2048]{1,0:T(8,128)(2,1)S(1)}, bf16[64,2048]{1,0:T(8,128)(2,1)S(1)}, u32[]{:S(2)}, u32[]{:S(2)}) collective-permute-start(bf16[64,2048]{1,0:T(8,128)(2,1)S(1)} %get-tuple-element.24), channel_id=1, source_target_pairs={{0,192},{64,0},{128,64},{192,128},{1,193},{65,1},{129,65},{193,129... | collective-permute-start | bytes 786440 | tf_op jit(solution)/shard_map/ppermute | solution.py:225
  12.7 0.0 collective-permute-start.2
  12.7 0.0 copy-done.5
  12.7 0.2 select_reduce_fusion
  12.8 3.3 %collective-permute-done.3.refs_2_ = bf16[64,2048]{1,0:T(8,128)(2,1)S(1)} collective-permute-done((bf16[64,2048]{1,0:T(8,128)(2,1)S(1)}, bf16[64,2048]{1,0:T(8,128)(2,1)S(1)}, u32[]{:S(2)}, u32[]{:S(2)}) %collective-permute-start.3) | collective-permute-done | bytes 262176 | tf_op jit(solution)/shard_map/ppermute | solution.py:219
  16.1 0.1 collective-permute-done.refs_0_
  16.3 5.5 %collective-permute-done.5.refs_3_ = bf16[64,2048]{1,0:T(8,128)(2,1)S(1)} collective-permute-done((bf16[64,2048]{1,0:T(8,128)(2,1)S(1)}, bf16[64,2048]{1,0:T(8,128)(2,1)S(1)}, u32[]{:S(2)}, u32[]{:S(2)}) %collective-permute-start.5) | collective-permute-done | bytes 262176 | tf_op jit(solution)/shard_map/ppermute | solution.py:225
  21.7 0.0 collective-permute-done.2.refs_1_
  21.7 0.2 combine.1
  22.0 29.4 %all_to_all.20 = bf16[64,4,8,128]{3,2,1,0:T(8,128)(2,1)S(1)} all-to-all(bf16[64,4,8,128]{3,2,1,0:T(8,128)(2,1)S(1)} %bitcast.38), channel_id=1, replica_groups={{40,41,42,43,44,45,46,47,32,33,34,35,36,37,38,39,56,57,58,59,60,61,62,6..., dimensions={0} | all-to-all | bytes 1048576 | tf_op jit(solution)/shard_map/all_to_all | solution.py:259
  51.3 0.0 copy-start.2
  51.3 0.0 copy-start.3
  51.3 1.0 to_slots.1
  52.3 41.8 %all_to_all.21 = bf16[256,2,8,128]{3,2,1,0:T(8,128)(2,1)S(1)} all-to-all(bf16[256,2,8,128]{3,2,1,0:T(8,128)(2,1)S(1)} %bitcast.35), channel_id=1, replica_groups=mesh['replica'=4,'shard'=64] {'replica','shard'}, dimensions={0} | all-to-all | bytes 2097152 | tf_op jit(solution)/shard_map/all_to_all | solution.py:269
  94.2 0.0 copy-start
  94.2 0.0 copy-done.2
  94.2 0.0 copy-done.3
  94.2 1.4 steer.1
  95.6 0.0 copy-done
  95.6 36.9 %all_to_all.22 = bf16[256,2,8,128]{3,2,1,0:T(8,128)(2,1)S(1)} all-to-all(bf16[256,2,8,128]{3,2,1,0:T(8,128)(2,1)S(1)} %bitcast.37), channel_id=1, replica_groups=mesh['replica'=4,'shard'=64] {'replica','shard'}, dimensions={0} | all-to-all | bytes 2097152 | tf_op jit(solution)/shard_map/all_to_all | solution.py:278
  132.5 1.5 pick.1
  134.0 5.2 %all-to-all-start.3 = ((bf16[256,8,128]{2,1,0:T(8,128)(2,1)}), bf16[256,8,128]{2,1,0:T(8,128)(2,1)S(1)}, u32[]{:S(2)}, u32[]{:S(2)}) async-start(bf16[256,8,128]{2,1,0:T(8,128)(2,1)} %pick.1), calls=%async_computation.3 | async-start | bytes 1048576 | tf_op jit(solution)/shard_map/all_to_all | solution.py:286
  139.2 5.4 %gram.1 = (f32[2,512,512]{2,1,0:T(8,128)}, f32[2,512,512]{2,1,0:T(8,128)}) custom-call(bf16[64,4,2,8,128]{4,3,2,1,0:T(8,128)(2,1)} %bitcast.30, f32[2,512,512]{2,1,0:T(8,128)} %left_ref.2, f32[2,512,512]{2,1,0:T(8,128)} %right_ref.2), custom_call_target="tpu_custom_call" | custom-call | flops 1073741824 | bytes 9437184 | tf_op jit(solution)/shard_map/gram/pallas_call | solution.py:186
  144.6 14.4 %all-to-all-done.3 = bf16[256,8,128]{2,1,0:T(8,128)(2,1)S(1)} async-done(((bf16[256,8,128]{2,1,0:T(8,128)(2,1)}), bf16[256,8,128]{2,1,0:T(8,128)(2,1)S(1)}, u32[]{:S(2)}, u32[]{:S(2)}) %all-to-all-start.3) | async-done | bytes 524320 | tf_op jit(solution)/shard_map/all_to_all | solution.py:286
  159.0 0.8 copy.11
  (3 shorter events, 0.0 us)
Async XLA Ops:
  0.6 9.9 %copy-start.1 = (bf16[1,512,2048]{2,1,0:T(8,128)(2,1)S(1)}, bf16[1,512,2048]{2,1,0:T(8,128)(2,1)}, u32[]{:S(2)}) copy-start(bf16[1,512,2048]{2,1,0:T(8,128)(2,1)} %param.7) | copy-start | bytes 6291460
  0.6 7.3 %copy-start.4 = (s32[256,2]{0,1:T(2,128)S(1)}, s32[256,2]{0,1:T(2,128)}, u32[]{:S(2)}) copy-start(s32[256,2]{0,1:T(2,128)} %param.9) | copy-start | bytes 6148
  0.7 12.0 %copy-start.5 = (s32[256]{0:T(256)S(1)}, s32[256]{0:T(256)}, u32[]{:S(2)}) copy-start(s32[256]{0:T(256)} %param.8) | copy-start | bytes 3076
  1.9 7.1 %collective-permute-start.1 = (bf16[64,2048]{1,0:T(8,128)(2,1)S(1)}, bf16[64,2048]{1,0:T(8,128)(2,1)S(1)}, u32[]{:S(2)}, u32[]{:S(2)}) collective-permute-start(bf16[64,2048]{1,0:T(8,128)(2,1)S(1)} %get-tuple-element.12), channel_id=1, source_target_pairs={{0,64},{64,128},{128,192},{192,0},{1,65},{65,129},{129,193},{193,1... | collective-permute-start | bytes 786440 | tf_op jit(solution)/shard_map/ppermute | solution.py:216
  4.0 6.5 %collective-permute-start.4 = (bf16[64,2048]{1,0:T(8,128)(2,1)S(1)}, bf16[64,2048]{1,0:T(8,128)(2,1)S(1)}, u32[]{:S(2)}, u32[]{:S(2)}) collective-permute-start(bf16[64,2048]{1,0:T(8,128)(2,1)S(1)} %get-tuple-element.13), channel_id=1, source_target_pairs={{0,192},{64,0},{128,64},{192,128},{1,193},{65,1},{129,65},{193,129... | collective-permute-start | bytes 786440 | tf_op jit(solution)/shard_map/ppermute | solution.py:217
  6.4 9.7 %collective-permute-start.3 = (bf16[64,2048]{1,0:T(8,128)(2,1)S(1)}, bf16[64,2048]{1,0:T(8,128)(2,1)S(1)}, u32[]{:S(2)}, u32[]{:S(2)}) collective-permute-start(bf16[64,2048]{1,0:T(8,128)(2,1)S(1)} %get-tuple-element.26), channel_id=1, source_target_pairs={{0,192},{64,0},{128,64},{192,128},{1,193},{65,1},{129,65},{193,129... | collective-permute-start | bytes 786440 | tf_op jit(solution)/shard_map/ppermute | solution.py:219
  7.9 8.4 %collective-permute-start = (bf16[64,2048]{1,0:T(8,128)(2,1)S(1)}, bf16[64,2048]{1,0:T(8,128)(2,1)S(1)}, u32[]{:S(2)}, u32[]{:S(2)}) collective-permute-start(bf16[64,2048]{1,0:T(8,128)(2,1)S(1)} %get-tuple-element.27), channel_id=1, source_target_pairs={{0,64},{64,128},{128,192},{192,0},{1,65},{65,129},{129,193},{193,1... | collective-permute-start | bytes 786440 | tf_op jit(solution)/shard_map/ppermute | solution.py:218
  10.6 11.1 %collective-permute-start.5 = (bf16[64,2048]{1,0:T(8,128)(2,1)S(1)}, bf16[64,2048]{1,0:T(8,128)(2,1)S(1)}, u32[]{:S(2)}, u32[]{:S(2)}) collective-permute-start(bf16[64,2048]{1,0:T(8,128)(2,1)S(1)} %get-tuple-element.24), channel_id=1, source_target_pairs={{0,192},{64,0},{128,64},{192,128},{1,193},{65,1},{129,65},{193,129... | collective-permute-start | bytes 786440 | tf_op jit(solution)/shard_map/ppermute | solution.py:225
  12.7 9.1 %collective-permute-start.2 = (bf16[64,2048]{1,0:T(8,128)(2,1)S(1)}, bf16[64,2048]{1,0:T(8,128)(2,1)S(1)}, u32[]{:S(2)}, u32[]{:S(2)}) collective-permute-start(bf16[64,2048]{1,0:T(8,128)(2,1)S(1)} %get-tuple-element.25), channel_id=1, source_target_pairs={{0,64},{64,128},{128,192},{192,0},{1,65},{65,129},{129,193},{193,1... | collective-permute-start | bytes 786440 | tf_op jit(solution)/shard_map/ppermute | solution.py:224
  51.3 42.8 %copy-start.2 = (bf16[2,512,512]{2,1,0:T(8,128)(2,1)S(1)}, bf16[2,512,512]{2,1,0:T(8,128)(2,1)}, u32[]{:S(2)}) copy-start(bf16[2,512,512]{2,1,0:T(8,128)(2,1)} %left_ref.3) | copy-start | bytes 3145732
  51.3 42.8 %copy-start.3 = (bf16[2,512,512]{2,1,0:T(8,128)(2,1)S(1)}, bf16[2,512,512]{2,1,0:T(8,128)(2,1)}, u32[]{:S(2)}) copy-start(bf16[2,512,512]{2,1,0:T(8,128)(2,1)} %right_ref.3) | copy-start | bytes 3145732
  94.2 1.4 copy-start
  134.0 25.0 %all-to-all-start.3 = ((bf16[256,8,128]{2,1,0:T(8,128)(2,1)}), bf16[256,8,128]{2,1,0:T(8,128)(2,1)S(1)}, u32[]{:S(2)}, u32[]{:S(2)}) async-start(bf16[256,8,128]{2,1,0:T(8,128)(2,1)} %pick.1), calls=%async_computation.3 | async-start | bytes 1048576 | tf_op jit(solution)/shard_map/all_to_all | solution.py:286

commit v5 on v4

--- a/solution.py
+++ b/solution.py
@@ -11,8 +11,8 @@
 LANES = 128
 UNROLL = 32
 PARTS = 4
-FAR_SHARD = 40
-FAR_DEVICE = 168
+FAR_SHARD = 41
+FAR_DEVICE = 169
 STRIDE = 2
 VMEM_LIMIT = 16 * 1024 * 1024
 GRAM_VMEM = 62 * 1024 * 1024
@@ -39,7 +39,7 @@
                 ).astype(out_ref.dtype)
                 for group in range(groups):
                     row = (side * groups + group) ^ (FAR_SHARD // across)
-                    out_ref[row, tile, block] = total[group * ROWS : (group + 1) * ROWS]
+                    out_ref[row, tile ^ (FAR_SHARD % across), block] = total[group * ROWS : (group + 1) * ROWS]
 
 
 def combine(me, parts, right_plain, right_sum, left_plain, left_sum, ncols):
@@ -133,7 +133,7 @@
             piece = steer[:, tile * LANES : (tile + 1) * LANES].reshape(groups, ROWS, LANES)
             for group in range(0, groups, STRIDE):
                 rows = pl.ds(group ^ (FAR_DEVICE // across), STRIDE)
-                out_ref[rows, tile, slot] = piece[group : group + STRIDE]
+                out_ref[rows, tile ^ (FAR_DEVICE % across), slot] = piece[group : group + STRIDE]
 
 
 def gram_kernel(tiles_ref, left_ref, right_ref, new_left_ref, new_right_ref, held, in_sems, out_sems):

time: 160 us -> 159 us (level)
  no operation moved by 1% of the time
where the time goes in v5:
time: 159 us
  blocking collectives  108 us (68%)
  waiting for transfers between devices  25.4 us (16%)
  starting transfers between devices  12.2 us (8%)
  Pallas kernels  9.51 us (6%)
  local copies, waits for them, and re-layouts  3.1 us (2%)
    all_to_all x1, blocking collectives, on_device(): lax.all_to_all(by_slot.reshape(devices, slots, ROWS, LANES), everyone, sp...  41.7 us
    all_to_all x1, blocking collectives, on_device(): lax.all_to_all(steer.reshape(devices, slots, ROWS, LANES), everyone, spli...  36.9 us
    all_to_all x1, blocking collectives, on_device(): lax.all_to_all(summed.reshape(shards, ncols, ROWS, LANES), 'shard', split...  28.9 us
    all_to_all x1, waiting for transfers between devices, on_device(): lax.all_to_all(by_place, everyone, split_axis=0, concat_axis=0, axis_inde...  14 us
    ppermute x1, waiting for transfers between devices, reduce_rows(): left_sum = lax.ppermute(add(part(3, 1), from_right), 'replica', leftward)  5.47 us
    pallas_call x1, Pallas kernels, gram_slots(): pl.pallas_call(gram_kernel, out_shape=[jax.ShapeDtypeStruct(stat.shape, s...  5.37 us
    all_to_all x1, starting transfers between devices, on_device(): lax.all_to_all(by_place, everyone, split_axis=0, concat_axis=0, axis_inde...  5.19 us
    ppermute x1, waiting for transfers between devices, reduce_rows(): left_plain = lax.ppermute(part(3, 0), 'replica', leftward)  3.3 us
  transfers between devices with their start and end apart: 7, of which 6 were waited for; matrix products, arithmetic and copies ran while one was open for 1% of the time, Pallas kernels for 3%

profile of v5, /device:TPU:1, one launch (start us, length us, event | category | flops | bytes accessed | tf_op | source)
XLA Modules:
  0.0 158.8 jit_solution(9720165061735104500)
XLA Ops:
  0.6 0.0 copy-start.1
  0.6 0.0 copy-start.4
  0.7 0.0 copy-start.5
  0.7 1.2 dynamic-slice_bitcast_fusion.2
  1.9 2.1 %collective-permute-start.1 = (bf16[64,2048]{1,0:T(8,128)(2,1)S(1)}, bf16[64,2048]{1,0:T(8,128)(2,1)S(1)}, u32[]{:S(2)}, u32[]{:S(2)}) collective-permute-start(bf16[64,2048]{1,0:T(8,128)(2,1)S(1)} %get-tuple-element.12), channel_id=1, source_target_pairs={{0,64},{64,128},{128,192},{192,0},{1,65},{65,129},{129,193},{193,1... | collective-permute-start | bytes 786440 | tf_op jit(solution)/shard_map/ppermute | solution.py:216
  4.0 1.4 collective-permute-start.4
  5.4 1.1 dynamic-slice_bitcast_fusion
  6.4 1.5 collective-permute-start.3
  7.9 0.1 collective-permute-start
  8.0 0.0 copy-done.4
  8.0 1.0 collective-permute-done.1
  9.0 1.5 collective-permute-done.4
  10.5 0.0 copy-done.1
  10.5 0.1 fusion
  10.6 2.0 %collective-permute-start.5 = (bf16[64,2048]{1,0:T(8,128)(2,1)S(1)}, bf16[64,2048]{1,0:T(8,128)(2,1)S(1)}, u32[]{:S(2)}, u32[]{:S(2)}) collective-permute-start(bf16[64,2048]{1,0:T(8,128)(2,1)S(1)} %get-tuple-element.24), channel_id=1, source_target_pairs={{0,192},{64,0},{128,64},{192,128},{1,193},{65,1},{129,65},{193,129... | collective-permute-start | bytes 786440 | tf_op jit(solution)/shard_map/ppermute | solution.py:225
  12.7 0.0 collective-permute-start.2
  12.7 0.0 copy-done.5
  12.7 0.2 select_reduce_fusion
  12.8 3.3 %collective-permute-done.3.refs_2_ = bf16[64,2048]{1,0:T(8,128)(2,1)S(1)} collective-permute-done((bf16[64,2048]{1,0:T(8,128)(2,1)S(1)}, bf16[64,2048]{1,0:T(8,128)(2,1)S(1)}, u32[]{:S(2)}, u32[]{:S(2)}) %collective-permute-start.3) | collective-permute-done | bytes 262176 | tf_op jit(solution)/shard_map/ppermute | solution.py:219
  16.1 0.1 collective-permute-done.refs_0_
  16.3 5.5 %collective-permute-done.5.refs_3_ = bf16[64,2048]{1,0:T(8,128)(2,1)S(1)} collective-permute-done((bf16[64,2048]{1,0:T(8,128)(2,1)S(1)}, bf16[64,2048]{1,0:T(8,128)(2,1)S(1)}, u32[]{:S(2)}, u32[]{:S(2)}) %collective-permute-start.5) | collective-permute-done | bytes 262176 | tf_op jit(solution)/shard_map/ppermute | solution.py:225
  21.7 0.0 collective-permute-done.2.refs_1_
  21.7 0.2 combine.1
  22.0 28.9 %all_to_all.20 = bf16[64,4,8,128]{3,2,1,0:T(8,128)(2,1)S(1)} all-to-all(bf16[64,4,8,128]{3,2,1,0:T(8,128)(2,1)S(1)} %bitcast.38), channel_id=1, replica_groups={{41,40,43,42,45,44,47,46,33,32,35,34,37,36,39,38,57,56,59,58,61,60,63,6..., dimensions={0} | all-to-all | bytes 1048576 | tf_op jit(solution)/shard_map/all_to_all | solution.py:259
  50.9 0.0 copy-start.2
  50.9 0.0 copy-start.3
  50.9 1.0 to_slots.1
  51.9 41.7 %all_to_all.21 = bf16[256,2,8,128]{3,2,1,0:T(8,128)(2,1)S(1)} all-to-all(bf16[256,2,8,128]{3,2,1,0:T(8,128)(2,1)S(1)} %bitcast.35), channel_id=1, replica_groups=mesh['replica'=4,'shard'=64] {'replica','shard'}, dimensions={0} | all-to-all | bytes 2097152 | tf_op jit(solution)/shard_map/all_to_all | solution.py:269
  93.6 0.0 copy-start
  93.6 0.0 copy-done.2
  93.6 0.0 copy-done.3
  93.6 1.4 steer.1
  95.0 0.0 copy-done
  95.0 36.9 %all_to_all.22 = bf16[256,2,8,128]{3,2,1,0:T(8,128)(2,1)S(1)} all-to-all(bf16[256,2,8,128]{3,2,1,0:T(8,128)(2,1)S(1)} %bitcast.37), channel_id=1, replica_groups=mesh['replica'=4,'shard'=64] {'replica','shard'}, dimensions={0} | all-to-all | bytes 2097152 | tf_op jit(solution)/shard_map/all_to_all | solution.py:278
  131.9 1.5 pick.1
  133.4 5.2 %all-to-all-start.3 = ((bf16[256,8,128]{2,1,0:T(8,128)(2,1)}), bf16[256,8,128]{2,1,0:T(8,128)(2,1)S(1)}, u32[]{:S(2)}, u32[]{:S(2)}) async-start(bf16[256,8,128]{2,1,0:T(8,128)(2,1)} %pick.1), calls=%async_computation.3 | async-start | bytes 1048576 | tf_op jit(solution)/shard_map/all_to_all | solution.py:286
  138.6 5.4 %gram.1 = (f32[2,512,512]{2,1,0:T(8,128)}, f32[2,512,512]{2,1,0:T(8,128)}) custom-call(bf16[64,4,2,8,128]{4,3,2,1,0:T(8,128)(2,1)} %bitcast.30, f32[2,512,512]{2,1,0:T(8,128)} %left_ref.2, f32[2,512,512]{2,1,0:T(8,128)} %right_ref.2), custom_call_target="tpu_custom_call" | custom-call | flops 1073741824 | bytes 9437184 | tf_op jit(solution)/shard_map/gram/pallas_call | solution.py:186
  144.0 14.0 %all-to-all-done.3 = bf16[256,8,128]{2,1,0:T(8,128)(2,1)S(1)} async-done(((bf16[256,8,128]{2,1,0:T(8,128)(2,1)}), bf16[256,8,128]{2,1,0:T(8,128)(2,1)S(1)}, u32[]{:S(2)}, u32[]{:S(2)}) %all-to-all-start.3) | async-done | bytes 524320 | tf_op jit(solution)/shard_map/all_to_all | solution.py:286
  158.0 0.8 copy.11
  (3 shorter events, 0.0 us)
Async XLA Ops:
  0.6 9.9 %copy-start.1 = (bf16[1,512,2048]{2,1,0:T(8,128)(2,1)S(1)}, bf16[1,512,2048]{2,1,0:T(8,128)(2,1)}, u32[]{:S(2)}) copy-start(bf16[1,512,2048]{2,1,0:T(8,128)(2,1)} %param.7) | copy-start | bytes 6291460
  0.6 7.3 %copy-start.4 = (s32[256,2]{0,1:T(2,128)S(1)}, s32[256,2]{0,1:T(2,128)}, u32[]{:S(2)}) copy-start(s32[256,2]{0,1:T(2,128)} %param.9) | copy-start | bytes 6148
  0.7 12.0 %copy-start.5 = (s32[256]{0:T(256)S(1)}, s32[256]{0:T(256)}, u32[]{:S(2)}) copy-start(s32[256]{0:T(256)} %param.8) | copy-start | bytes 3076
  1.9 7.1 %collective-permute-start.1 = (bf16[64,2048]{1,0:T(8,128)(2,1)S(1)}, bf16[64,2048]{1,0:T(8,128)(2,1)S(1)}, u32[]{:S(2)}, u32[]{:S(2)}) collective-permute-start(bf16[64,2048]{1,0:T(8,128)(2,1)S(1)} %get-tuple-element.12), channel_id=1, source_target_pairs={{0,64},{64,128},{128,192},{192,0},{1,65},{65,129},{129,193},{193,1... | collective-permute-start | bytes 786440 | tf_op jit(solution)/shard_map/ppermute | solution.py:216
  4.0 6.5 %collective-permute-start.4 = (bf16[64,2048]{1,0:T(8,128)(2,1)S(1)}, bf16[64,2048]{1,0:T(8,128)(2,1)S(1)}, u32[]{:S(2)}, u32[]{:S(2)}) collective-permute-start(bf16[64,2048]{1,0:T(8,128)(2,1)S(1)} %get-tuple-element.13), channel_id=1, source_target_pairs={{0,192},{64,0},{128,64},{192,128},{1,193},{65,1},{129,65},{193,129... | collective-permute-start | bytes 786440 | tf_op jit(solution)/shard_map/ppermute | solution.py:217
  6.4 9.7 %collective-permute-start.3 = (bf16[64,2048]{1,0:T(8,128)(2,1)S(1)}, bf16[64,2048]{1,0:T(8,128)(2,1)S(1)}, u32[]{:S(2)}, u32[]{:S(2)}) collective-permute-start(bf16[64,2048]{1,0:T(8,128)(2,1)S(1)} %get-tuple-element.26), channel_id=1, source_target_pairs={{0,192},{64,0},{128,64},{192,128},{1,193},{65,1},{129,65},{193,129... | collective-permute-start | bytes 786440 | tf_op jit(solution)/shard_map/ppermute | solution.py:219
  7.9 8.4 %collective-permute-start = (bf16[64,2048]{1,0:T(8,128)(2,1)S(1)}, bf16[64,2048]{1,0:T(8,128)(2,1)S(1)}, u32[]{:S(2)}, u32[]{:S(2)}) collective-permute-start(bf16[64,2048]{1,0:T(8,128)(2,1)S(1)} %get-tuple-element.27), channel_id=1, source_target_pairs={{0,64},{64,128},{128,192},{192,0},{1,65},{65,129},{129,193},{193,1... | collective-permute-start | bytes 786440 | tf_op jit(solution)/shard_map/ppermute | solution.py:218
  10.6 11.1 %collective-permute-start.5 = (bf16[64,2048]{1,0:T(8,128)(2,1)S(1)}, bf16[64,2048]{1,0:T(8,128)(2,1)S(1)}, u32[]{:S(2)}, u32[]{:S(2)}) collective-permute-start(bf16[64,2048]{1,0:T(8,128)(2,1)S(1)} %get-tuple-element.24), channel_id=1, source_target_pairs={{0,192},{64,0},{128,64},{192,128},{1,193},{65,1},{129,65},{193,129... | collective-permute-start | bytes 786440 | tf_op jit(solution)/shard_map/ppermute | solution.py:225
  12.7 9.1 %collective-permute-start.2 = (bf16[64,2048]{1,0:T(8,128)(2,1)S(1)}, bf16[64,2048]{1,0:T(8,128)(2,1)S(1)}, u32[]{:S(2)}, u32[]{:S(2)}) collective-permute-start(bf16[64,2048]{1,0:T(8,128)(2,1)S(1)} %get-tuple-element.25), channel_id=1, source_target_pairs={{0,64},{64,128},{128,192},{192,0},{1,65},{65,129},{129,193},{193,1... | collective-permute-start | bytes 786440 | tf_op jit(solution)/shard_map/ppermute | solution.py:224
  50.9 42.7 %copy-start.2 = (bf16[2,512,512]{2,1,0:T(8,128)(2,1)S(1)}, bf16[2,512,512]{2,1,0:T(8,128)(2,1)}, u32[]{:S(2)}) copy-start(bf16[2,512,512]{2,1,0:T(8,128)(2,1)} %left_ref.3) | copy-start | bytes 3145732
  50.9 42.7 %copy-start.3 = (bf16[2,512,512]{2,1,0:T(8,128)(2,1)S(1)}, bf16[2,512,512]{2,1,0:T(8,128)(2,1)}, u32[]{:S(2)}) copy-start(bf16[2,512,512]{2,1,0:T(8,128)(2,1)} %right_ref.3) | copy-start | bytes 3145732
  93.6 1.4 copy-start
  133.4 24.6 %all-to-all-start.3 = ((bf16[256,8,128]{2,1,0:T(8,128)(2,1)}), bf16[256,8,128]{2,1,0:T(8,128)(2,1)S(1)}, u32[]{:S(2)}, u32[]{:S(2)}) async-start(bf16[256,8,128]{2,1,0:T(8,128)(2,1)} %pick.1), calls=%async_computation.3 | async-start | bytes 1048576 | tf_op jit(solution)/shard_map/all_to_all | solution.py:286

commit v6 on v5

--- a/solution.py
+++ b/solution.py
@@ -208,21 +208,25 @@
     rightward = [(i, (i + 1) % replicas) for i in range(replicas)]
     leftward = [(i, (i - 1) % replicas) for i in range(replicas)]
 
-    def part(shift, side):
+    def part(shift, side, parts):
         index = lax.rem(me + shift, replicas)
         return lax.dynamic_slice(parts, (index, side, 0, 0), (1, 1, rows // 2, cols))[0, 0]
 
-    parts, far_right, far_left = lax.optimization_barrier((parts, part(2, 0), part(2, 1)))
+    parts, far_right, far_left = lax.optimization_barrier(
+        (parts, part(2, 0, parts), part(2, 1, parts))
+    )
     from_left = lax.ppermute(far_right, "replica", rightward)
     from_right = lax.ppermute(far_left, "replica", leftward)
-    right_plain = lax.ppermute(part(1, 1), "replica", rightward)
-    left_plain = lax.ppermute(part(3, 0), "replica", leftward)
+    right_plain = lax.ppermute(part(1, 1, parts), "replica", rightward)
+    left_plain = lax.ppermute(part(3, 0, parts), "replica", leftward)
 
     def add(first, second):
         return (first.astype(jnp.float32) + second.astype(jnp.float32)).astype(grads.dtype)
 
-    right_sum = lax.ppermute(add(part(1, 0), from_left), "replica", rightward)
-    left_sum = lax.ppermute(add(part(3, 1), from_right), "replica", leftward)
+    own, from_left = lax.optimization_barrier((parts, from_left))
+    right_sum = lax.ppermute(add(part(1, 0, own), from_left), "replica", rightward)
+    own, from_right = lax.optimization_barrier((parts, from_right))
+    left_sum = lax.ppermute(add(part(3, 1, own), from_right), "replica", leftward)
     return combine(
         jnp.reshape(me, (1,)).astype(jnp.int32),
         parts,
@@ -245,7 +249,6 @@
     groups = width // ROWS
     row = block_offsets[:, 0] // width
     col = block_offsets[:, 1] // width
-
 
     def owners_by(place):
         here = place[None, :] == jnp.arange(blocks, dtype=jnp.int32)[:, None]

time: 159 us -> 159 us (level)
  starting transfers between devices: 12.2 us -> 13.8 us
  transfers between devices with their start and end apart: 7 -> 7, of which waited for: 6 -> 5; matrix products, arithmetic and copies ran while one was open for 1% -> 1% of each run, Pallas kernels for 3% -> 3%
where the time goes in v6:
time: 159 us
  blocking collectives  107 us (67%)
  waiting for transfers between devices  24 us (15%)
  starting transfers between devices  13.8 us (9%)
  Pallas kernels  9.5 us (6%)
  local copies, waits for them, and re-layouts  3.1 us (2%)
    all_to_all x1, blocking collectives, on_device(): lax.all_to_all(by_slot.reshape(devices, slots, ROWS, LANES), everyone, sp...  42.7 us
    all_to_all x1, blocking collectives, on_device(): lax.all_to_all(steer.reshape(devices, slots, ROWS, LANES), everyone, spli...  36.9 us
    all_to_all x1, blocking collectives, on_device(): lax.all_to_all(summed.reshape(shards, ncols, ROWS, LANES), 'shard', split...  27.8 us
    all_to_all x1, waiting for transfers between devices, on_device(): lax.all_to_all(by_place, everyone, split_axis=0, concat_axis=0, axis_inde...  14 us
    ppermute x1, waiting for transfers between devices, reduce_rows(): lax.ppermute(add(part(1, 0, own), from_left), 'replica', rightward)  5.62 us
    pallas_call x1, Pallas kernels, gram_slots(): pl.pallas_call(gram_kernel, out_shape=[jax.ShapeDtypeStruct(stat.shape, s...  5.37 us
    all_to_all x1, starting transfers between devices, on_device(): lax.all_to_all(by_place, everyone, split_axis=0, concat_axis=0, axis_inde...  5.19 us
    ppermute x1, waiting for transfers between devices, reduce_rows(): left_plain = lax.ppermute(part(3, 0, parts), 'replica', leftward)  3.2 us
  transfers between devices with their start and end apart: 7, of which 5 were waited for; matrix products, arithmetic and copies ran while one was open for 1% of the time, Pallas kernels for 3%

profile of v6, /device:TPU:1, one launch (start us, length us, event | category | flops | bytes accessed | tf_op | source)
XLA Modules:
  0.0 158.8 jit_solution(9682779856474493884)
XLA Ops:
  0.6 0.0 copy-start.1
  0.6 0.0 copy-start.4
  0.7 0.0 copy-start.5
  0.7 1.2 dynamic-slice_bitcast_fusion.2
  1.9 2.1 %collective-permute-start.1 = (bf16[64,2048]{1,0:T(8,128)(2,1)S(1)}, bf16[64,2048]{1,0:T(8,128)(2,1)S(1)}, u32[]{:S(2)}, u32[]{:S(2)}) collective-permute-start(bf16[64,2048]{1,0:T(8,128)(2,1)S(1)} %get-tuple-element.16), channel_id=1, source_target_pairs={{0,64},{64,128},{128,192},{192,0},{1,65},{65,129},{129,193},{193,1... | collective-permute-start | bytes 786440 | tf_op jit(solution)/shard_map/ppermute | solution.py:218
  4.0 1.4 collective-permute-start.4
  5.4 1.1 dynamic-slice_bitcast_fusion
  6.4 1.5 collective-permute-start.3
  7.9 0.1 collective-permute-start
  8.0 0.0 copy-done.4
  8.0 1.0 collective-permute-done.1
  9.0 0.0 copy-done.1
  9.0 0.1 fusion.1
  9.1 1.9 %collective-permute-start.2 = (bf16[64,2048]{1,0:T(8,128)(2,1)S(1)}, bf16[64,2048]{1,0:T(8,128)(2,1)S(1)}, u32[]{:S(2)}, u32[]{:S(2)}) collective-permute-start(bf16[64,2048]{1,0:T(8,128)(2,1)S(1)} %fusion.1), channel_id=1, source_target_pairs={{0,64},{64,128},{128,192},{192,0},{1,65},{65,129},{129,193},{193,1... | collective-permute-start | bytes 786440 | tf_op jit(solution)/shard_map/ppermute | solution.py:227
  11.0 0.0 collective-permute-done.4
  11.0 0.1 fusion
  11.1 1.7 %collective-permute-start.5 = (bf16[64,2048]{1,0:T(8,128)(2,1)S(1)}, bf16[64,2048]{1,0:T(8,128)(2,1)S(1)}, u32[]{:S(2)}, u32[]{:S(2)}) collective-permute-start(bf16[64,2048]{1,0:T(8,128)(2,1)S(1)} %fusion), channel_id=1, source_target_pairs={{0,192},{64,0},{128,64},{192,128},{1,193},{65,1},{129,65},{193,129... | collective-permute-start | bytes 786440 | tf_op jit(solution)/shard_map/ppermute | solution.py:229
  12.8 0.0 copy-done.5
  12.8 0.1 select_reduce_fusion
  12.9 3.2 %collective-permute-done.3.refs_2_ = bf16[64,2048]{1,0:T(8,128)(2,1)S(1)} collective-permute-done((bf16[64,2048]{1,0:T(8,128)(2,1)S(1)}, bf16[64,2048]{1,0:T(8,128)(2,1)S(1)}, u32[]{:S(2)}, u32[]{:S(2)}) %collective-permute-start.3) | collective-permute-done | bytes 262176 | tf_op jit(solution)/shard_map/ppermute | solution.py:221
  16.1 0.1 collective-permute-done.refs_0_
  16.3 5.6 %collective-permute-done.2.refs_1_ = bf16[64,2048]{1,0:T(8,128)(2,1)S(1)} collective-permute-done((bf16[64,2048]{1,0:T(8,128)(2,1)S(1)}, bf16[64,2048]{1,0:T(8,128)(2,1)S(1)}, u32[]{:S(2)}, u32[]{:S(2)}) %collective-permute-start.2) | collective-permute-done | bytes 262176 | tf_op jit(solution)/shard_map/ppermute | solution.py:227
  21.9 0.0 collective-permute-done.5.refs_3_
  21.9 0.2 combine.1
  22.1 27.8 %all_to_all.20 = bf16[64,4,8,128]{3,2,1,0:T(8,128)(2,1)S(1)} all-to-all(bf16[64,4,8,128]{3,2,1,0:T(8,128)(2,1)S(1)} %bitcast.39), channel_id=1, replica_groups={{41,40,43,42,45,44,47,46,33,32,35,34,37,36,39,38,57,56,59,58,61,60,63,6..., dimensions={0} | all-to-all | bytes 1048576 | tf_op jit(solution)/shard_map/all_to_all | solution.py:262
  49.9 0.0 copy-start.2
  49.9 0.0 copy-start.3
  49.9 1.0 to_slots.1
  50.9 42.7 %all_to_all.21 = bf16[256,2,8,128]{3,2,1,0:T(8,128)(2,1)S(1)} all-to-all(bf16[256,2,8,128]{3,2,1,0:T(8,128)(2,1)S(1)} %bitcast.36), channel_id=1, replica_groups=mesh['replica'=4,'shard'=64] {'replica','shard'}, dimensions={0} | all-to-all | bytes 2097152 | tf_op jit(solution)/shard_map/all_to_all | solution.py:272
  93.6 0.0 copy-start
  93.6 0.0 copy-done.2
  93.6 0.0 copy-done.3
  93.6 1.4 steer.1
  95.0 0.0 copy-done
  95.0 36.9 %all_to_all.22 = bf16[256,2,8,128]{3,2,1,0:T(8,128)(2,1)S(1)} all-to-all(bf16[256,2,8,128]{3,2,1,0:T(8,128)(2,1)S(1)} %bitcast.38), channel_id=1, replica_groups=mesh['replica'=4,'shard'=64] {'replica','shard'}, dimensions={0} | all-to-all | bytes 2097152 | tf_op jit(solution)/shard_map/all_to_all | solution.py:281
  131.9 1.5 pick.1
  133.4 5.2 %all-to-all-start.3 = ((bf16[256,8,128]{2,1,0:T(8,128)(2,1)}), bf16[256,8,128]{2,1,0:T(8,128)(2,1)S(1)}, u32[]{:S(2)}, u32[]{:S(2)}) async-start(bf16[256,8,128]{2,1,0:T(8,128)(2,1)} %pick.1), calls=%async_computation.3 | async-start | bytes 1048576 | tf_op jit(solution)/shard_map/all_to_all | solution.py:289
  138.6 5.4 %gram.1 = (f32[2,512,512]{2,1,0:T(8,128)}, f32[2,512,512]{2,1,0:T(8,128)}) custom-call(bf16[64,4,2,8,128]{4,3,2,1,0:T(8,128)(2,1)} %bitcast.30, f32[2,512,512]{2,1,0:T(8,128)} %left_ref.2, f32[2,512,512]{2,1,0:T(8,128)} %right_ref.2), custom_call_target="tpu_custom_call" | custom-call | flops 1073741824 | bytes 9437184 | tf_op jit(solution)/shard_map/gram/pallas_call | solution.py:186
  144.0 14.0 %all-to-all-done.3 = bf16[256,8,128]{2,1,0:T(8,128)(2,1)S(1)} async-done(((bf16[256,8,128]{2,1,0:T(8,128)(2,1)}), bf16[256,8,128]{2,1,0:T(8,128)(2,1)S(1)}, u32[]{:S(2)}, u32[]{:S(2)}) %all-to-all-start.3) | async-done | bytes 524320 | tf_op jit(solution)/shard_map/all_to_all | solution.py:289
  158.0 0.8 copy.11
  (3 shorter events, 0.0 us)
Async XLA Ops:
  0.6 8.4 %copy-start.1 = (bf16[1,512,2048]{2,1,0:T(8,128)(2,1)S(1)}, bf16[1,512,2048]{2,1,0:T(8,128)(2,1)}, u32[]{:S(2)}) copy-start(bf16[1,512,2048]{2,1,0:T(8,128)(2,1)} %param.7) | copy-start | bytes 6291460
  0.6 7.3 %copy-start.4 = (s32[256,2]{0,1:T(2,128)S(1)}, s32[256,2]{0,1:T(2,128)}, u32[]{:S(2)}) copy-start(s32[256,2]{0,1:T(2,128)} %param.9) | copy-start | bytes 6148
  0.7 12.1 %copy-start.5 = (s32[256]{0:T(256)S(1)}, s32[256]{0:T(256)}, u32[]{:S(2)}) copy-start(s32[256]{0:T(256)} %param.8) | copy-start | bytes 3076
  1.9 7.1 %collective-permute-start.1 = (bf16[64,2048]{1,0:T(8,128)(2,1)S(1)}, bf16[64,2048]{1,0:T(8,128)(2,1)S(1)}, u32[]{:S(2)}, u32[]{:S(2)}) collective-permute-start(bf16[64,2048]{1,0:T(8,128)(2,1)S(1)} %get-tuple-element.16), channel_id=1, source_target_pairs={{0,64},{64,128},{128,192},{192,0},{1,65},{65,129},{129,193},{193,1... | collective-permute-start | bytes 786440 | tf_op jit(solution)/shard_map/ppermute | solution.py:218
  4.0 7.0 %collective-permute-start.4 = (bf16[64,2048]{1,0:T(8,128)(2,1)S(1)}, bf16[64,2048]{1,0:T(8,128)(2,1)S(1)}, u32[]{:S(2)}, u32[]{:S(2)}) collective-permute-start(bf16[64,2048]{1,0:T(8,128)(2,1)S(1)} %get-tuple-element.19), channel_id=1, source_target_pairs={{0,192},{64,0},{128,64},{192,128},{1,193},{65,1},{129,65},{193,129... | collective-permute-start | bytes 786440 | tf_op jit(solution)/shard_map/ppermute | solution.py:219
  6.4 9.7 %collective-permute-start.3 = (bf16[64,2048]{1,0:T(8,128)(2,1)S(1)}, bf16[64,2048]{1,0:T(8,128)(2,1)S(1)}, u32[]{:S(2)}, u32[]{:S(2)}) collective-permute-start(bf16[64,2048]{1,0:T(8,128)(2,1)S(1)} %get-tuple-element.32), channel_id=1, source_target_pairs={{0,192},{64,0},{128,64},{192,128},{1,193},{65,1},{129,65},{193,129... | collective-permute-start | bytes 786440 | tf_op jit(solution)/shard_map/ppermute | solution.py:221
  7.9 8.4 %collective-permute-start = (bf16[64,2048]{1,0:T(8,128)(2,1)S(1)}, bf16[64,2048]{1,0:T(8,128)(2,1)S(1)}, u32[]{:S(2)}, u32[]{:S(2)}) collective-permute-start(bf16[64,2048]{1,0:T(8,128)(2,1)S(1)} %get-tuple-element.33), channel_id=1, source_target_pairs={{0,64},{64,128},{128,192},{192,0},{1,65},{65,129},{129,193},{193,1... | collective-permute-start | bytes 786440 | tf_op jit(solution)/shard_map/ppermute | solution.py:220
  9.1 12.8 %collective-permute-start.2 = (bf16[64,2048]{1,0:T(8,128)(2,1)S(1)}, bf16[64,2048]{1,0:T(8,128)(2,1)S(1)}, u32[]{:S(2)}, u32[]{:S(2)}) collective-permute-start(bf16[64,2048]{1,0:T(8,128)(2,1)S(1)} %fusion.1), channel_id=1, source_target_pairs={{0,64},{64,128},{128,192},{192,0},{1,65},{65,129},{129,193},{193,1... | collective-permute-start | bytes 786440 | tf_op jit(solution)/shard_map/ppermute | solution.py:227
  11.1 10.8 %collective-permute-start.5 = (bf16[64,2048]{1,0:T(8,128)(2,1)S(1)}, bf16[64,2048]{1,0:T(8,128)(2,1)S(1)}, u32[]{:S(2)}, u32[]{:S(2)}) collective-permute-start(bf16[64,2048]{1,0:T(8,128)(2,1)S(1)} %fusion), channel_id=1, source_target_pairs={{0,192},{64,0},{128,64},{192,128},{1,193},{65,1},{129,65},{193,129... | collective-permute-start | bytes 786440 | tf_op jit(solution)/shard_map/ppermute | solution.py:229
  49.9 43.7 %copy-start.2 = (bf16[2,512,512]{2,1,0:T(8,128)(2,1)S(1)}, bf16[2,512,512]{2,1,0:T(8,128)(2,1)}, u32[]{:S(2)}) copy-start(bf16[2,512,512]{2,1,0:T(8,128)(2,1)} %left_ref.3) | copy-start | bytes 3145732
  49.9 43.7 %copy-start.3 = (bf16[2,512,512]{2,1,0:T(8,128)(2,1)S(1)}, bf16[2,512,512]{2,1,0:T(8,128)(2,1)}, u32[]{:S(2)}) copy-start(bf16[2,512,512]{2,1,0:T(8,128)(2,1)} %right_ref.3) | copy-start | bytes 3145732
  93.6 1.4 copy-start
  133.4 24.6 %all-to-all-start.3 = ((bf16[256,8,128]{2,1,0:T(8,128)(2,1)}), bf16[256,8,128]{2,1,0:T(8,128)(2,1)S(1)}, u32[]{:S(2)}, u32[]{:S(2)}) async-start(bf16[256,8,128]{2,1,0:T(8,128)(2,1)} %pick.1), calls=%async_computation.3 | async-start | bytes 1048576 | tf_op jit(solution)/shard_map/all_to_all | solution.py:289
